TPU v7x, 128 devices: a whole 4x4x4 slice. The times are simulated.
128 devices in a mesh: rows: 32 (over y, z, core), sub: 4 (over x).
Axes of the slice: x: 4, y: 4, z: 4, core: 2. Of those that a mesh axis runs over, the one named last changes fastest.
Arguments:
- vectors: bfloat16 [262144, 1024], P('rows'), may hold values from -6 to 6
- list_ids: int32 [262144], P('rows'), may hold values from 0 to 16383, as said below
- centroids: bfloat16 [16384, 1024], P(('rows', 'sub')), may hold values from -6 to 6
- rotation: bfloat16 [1024, 1024], P(None, 'sub'), may hold values from -0.1875 to 0.1875
- codes: int32 [64, 262144], P('sub', 'rows'), may hold values from 0 to 255, as said below
Outputs:
- codebooks: float32 [64, 256, 16], P('sub')
- cross_cov: float32 [1024, 1024], P('rows', 'sub')
Inputs may be any that keep to these rules, and one draw needn't show every extreme that they name: `codes`: every code 0 to 255 appears in every sub-space. `list_ids`: the coarse lists are held in consecutive blocks of 16384 // (32 * 4) by the devices in the order of rows+sub; the vectors of one index of rows name exactly 32 distinct lists of every such block.
All inputs are finite; a program needn't handle non-finite values.
Results may differ from a plain program's by a relative error of at most 0.0047.
Values may be sent and summed in bfloat16 or wider, within the bound.
A program may use at most 192 MiB of HBM per device.

v0:
```python
import jax
import jax.numpy as jnp
from jax import lax
from jax.sharding import PartitionSpec as P

KS = 256


def local(vectors, list_ids, centroids, rotation, codes):
    local_rows = vectors.shape[0]
    sub_width = rotation.shape[1]
    centre_table = lax.all_gather(centroids, ("rows", "sub"), axis=0, tiled=True)
    fetched = jnp.take(centre_table, list_ids, axis=0)
    residual = (vectors.astype(jnp.float32) - fetched.astype(jnp.float32)).astype(jnp.bfloat16)
    rotated = jnp.dot(residual, rotation, preferred_element_type=jnp.float32).astype(jnp.bfloat16)
    local_subs = codes.shape[0]
    space_width = sub_width // local_subs
    pieces = rotated.reshape(local_rows, local_subs, space_width)
    block_rows = min(1024, local_rows)
    block_count = local_rows // block_rows
    code_range = jnp.arange(KS, dtype=jnp.int32)

    def accumulate(carry, step_index):
        code_sums, counts = carry
        code_block = lax.dynamic_slice_in_dim(codes, step_index * block_rows, block_rows, 1)
        piece_block = lax.dynamic_slice_in_dim(pieces, step_index * block_rows, block_rows, 0)
        onehot = (code_block[:, :, None] == code_range[None, None, :]).astype(jnp.bfloat16)
        code_sums = code_sums + jnp.einsum(
            "mrk,rmd->mkd", onehot, piece_block, preferred_element_type=jnp.float32
        )
        counts = counts + jnp.sum(onehot, axis=1, dtype=jnp.float32)
        return ((code_sums, counts), None)

    start_sums = jnp.zeros((local_subs, KS, space_width), jnp.float32)
    start_counts = jnp.zeros((local_subs, KS), jnp.float32)
    (code_sums, counts), _ = lax.scan(
        accumulate, (start_sums, start_counts), jnp.arange(block_count, dtype=jnp.int32)
    )
    code_sums, counts = lax.psum((code_sums, counts), "rows")
    codebooks = code_sums / counts[:, :, None]
    book_rounded = codebooks.astype(jnp.bfloat16)

    def rebuild_block(step_index):
        code_block = lax.dynamic_slice_in_dim(codes, step_index * block_rows, block_rows, 1)
        onehot = (code_block[:, :, None] == code_range[None, None, :]).astype(jnp.bfloat16)
        picked = jnp.einsum(
            "mrk,mkd->rmd", onehot, book_rounded, preferred_element_type=jnp.float32
        )
        return picked.reshape(block_rows, sub_width).astype(jnp.bfloat16)

    rebuilt = lax.map(rebuild_block, jnp.arange(block_count, dtype=jnp.int32)).reshape(
        local_rows, sub_width
    )
    cross_cov = lax.psum_scatter(
        jnp.dot(residual.T, rebuilt, preferred_element_type=jnp.float32) / KS,
        "rows",
        scatter_dimension=0,
        tiled=True,
    )
    return (codebooks, cross_cov)


def solution(mesh):
    placed = (
        P("rows", None),
        P("rows"),
        P(("rows", "sub"), None),
        P(None, "sub"),
        P("sub", "rows"),
    )
    return jax.shard_map(
        local,
        mesh=mesh,
        in_specs=placed,
        out_specs=(P("sub", None, None), P("rows", "sub")),
        check_vma=False,
    )
```

profile of v0, /device:TPU:7, one launch (start us, length us, event | category | flops | bytes accessed | tf_op | source)
XLA Modules:
  0.0 654.7 jit_solution(16677715811727153327)
XLA Ops:
  9.5 111.1 %all-gather.2.cloned.1.call-done = bf16[16384,1024]{1,0:T(8,128)(2,1)} async-done(((bf16[128,1024]{1,0:T(8,128)(2,1)}), bf16[16384,1024]{1,0:T(8,128)(2,1)}) %all-gather.2.cloned.1.call-update) | async-done | bytes 33554448 | tf_op jit(solution)/shard_map/all_gather | solution.py:12
  120.7 150.0 %gather_fusion = bf16[8192,1024]{1,0:T(8,128)(2,1)} fusion(bf16[16384,1024]{1,0:T(8,128)(2,1)} %all-gather.2.cloned.1.call-done, s32[8192]{0:T(1024)S(1)} %fusion.13), kind=kCustom, calls=%fused_computation | custom fusion | bytes 33587200 | tf_op jit(solution)/shard_map/jit(_take)/gather | solution.py:13
  270.7 15.7 %convolution_convert_fusion = bf16[8192,256]{0,1:T(8,128)(2,1)} fusion(bf16[1024,256]{1,0:T(8,128)(2,1)S(1)} %copy-done, bf16[8192,1024]{1,0:T(8,128)(2,1)} %param.9, bf16[8192,1024]{1,0:T(8,128)(2,1)} %gather_fusion, pred[8192]{0:T(1024)(128)(4,1)S(1)} %compare_and_fusion), kind=kOutput, calls=%fused_computation.20 | convolution fusion | flops 4339007488 | bytes 38281216 | tf_op jit(solution)/shard_map/dot_general | solution.py:15
  286.4 86.5 %while.25 = (s32[]{:T(128)}, f32[16,256,16]{1,2,0:T(8,128)S(1)}, f32[16,256]{1,0:T(8,128)S(1)}, s32[8]{0:T(128)S(1)}, s32[16,8192]{1,0:T(8,128)}, /*index=5*/bf1...) while((s32[]{:T(128)}, f32[16,256,16]{1,2,0:T(8,128)S(1)}, ...), condition=%wide.region_2.3_spmd.clone, body=%wide.region_0.0_spmd.clone.sunk | while | flops 155324416 | bytes 1376434 | solution.py:36
  288.5 5.9 fusion.25
  294.3 2.8 convert_reduce_fusion.2
  299.3 5.9 fusion.25
  305.2 2.8 convert_reduce_fusion.2
  310.1 5.9 fusion.25
  316.0 2.8 convert_reduce_fusion.2
  320.9 5.9 fusion.25
  326.8 2.8 convert_reduce_fusion.2
  331.7 5.9 fusion.25
  337.6 2.8 convert_reduce_fusion.2
  342.5 5.9 fusion.25
  348.4 2.8 convert_reduce_fusion.2
  353.4 5.9 fusion.25
  359.2 2.8 convert_reduce_fusion.2
  364.2 5.9 fusion.25
  370.0 2.8 convert_reduce_fusion.2
  373.7 121.2 %psum.15 = f32[16,256]{1,0:T(8,128)S(1)} all-reduce(f32[16,256]{1,0:T(8,128)S(1)} %get-tuple-element.73), channel_id=1, replica_groups=mesh['rows'=32,'sub'=4] {'rows'}, use_global_device_ids=true, to_apply=%region_4.5 | all-reduce | flops 4096 | bytes 32768 | tf_op jit(solution)/shard_map/psum | solution.py:39
  496.6 56.3 %while.24 = (s32[]{:T(128)}, bf16[8,1024,256]{2,1,0:T(8,128)(2,1)}, s32[8]{0:T(128)S(1)}, s32[16,8192]{1,0:T(8,128)}, bf16[16,256,16]{1,2,0:T(8,128)(2,1)S(1)}, ...) while((s32[]{:T(128)}, bf16[8,1024,256]{2,1,0:T(8,128)(2,1)}, s32[8]{0:T(128)S(1)}, ...), condition=%wide.region_6.7_spmd.clone, body=%wide.region_5.6_spmd.clone.sunk | while | flops 138674176 | bytes 2949787 | solution.py:51
  498.6 4.0 fusion.23
  505.6 4.0 fusion.23
  512.7 4.0 fusion.23
  519.7 4.0 fusion.23
  526.7 4.0 fusion.23
  533.8 4.0 fusion.23
  540.8 4.0 fusion.23
  547.9 4.0 fusion.23
  552.9 17.8 %convolution_multiply_fusion = f32[1024,256]{1,0:T(8,128)} fusion(bf16[8192,256]{1,0:T(8,128)(2,1)} %bitcast.19, bf16[8192,1024]{1,0:T(8,128)(2,1)} %param.9, bf16[8192,1024]{1,0:T(8,128)(2,1)} %gather_fusion, pred[8192]{0:T(1024)(128)(4,1)S(1)} %compare_and_fusion), kind=kOutput, calls=%fused_computation.21 | convolution fusion | flops 4337172480 | bytes 38805504 | tf_op jit(solution)/shard_map/dot_general | solution.py:55
  570.7 77.4 %reduce-scatter.2.cloned.1.call-done = f32[32,256]{1,0:T(8,128)} async-done(((f32[1024,256]{1,0:T(8,128)}), f32[32,256]{1,0:T(8,128)}) %reduce-scatter.2.cloned.1.call-update) | async-done | bytes 32784 | tf_op jit(solution)/shard_map/reduce_scatter | solution.py:54
  (77 shorter events, 36.1 us)
Async XLA Ops:
  7.2 263.5 %copy-start = (bf16[1024,256]{1,0:T(8,128)(2,1)S(1)}, bf16[1024,256]{1,0:T(8,128)(2,1)}, u32[]{:S(2)}) copy-start(bf16[1024,256]{1,0:T(8,128)(2,1)} %param.12) | copy-start | bytes 1572868
  7.2 113.5 %all-gather.2.cloned.1.call-start = ((), (), s32[]{:S(2)}) async-start(), calls=%async_computation.1 | async-start | bytes 33816576 | tf_op jit(solution)/shard_map/all_gather | solution.py:12
  7.9 487.0 %all-reduce.2.cloned.1.call-start = ((), (), s32[]{:S(2)}) async-start(), calls=%async_computation.2 | async-start | bytes 524288 | tf_op jit(solution)/shard_map/psum | solution.py:39
  372.9 0.7 copy-start.2
  373.6 274.5 %reduce-scatter.2.cloned.1.call-start = ((), (), s32[]{:S(2)}) async-start(), calls=%async_computation.3 | async-start | bytes 1081344 | tf_op jit(solution)/shard_map/reduce_scatter | solution.py:54
  552.9 95.2 %copy-start.1 = (bf16[1024,256]{1,0:T(8,128)(2,1)S(1)}, bf16[1024,256]{1,0:T(8,128)(2,1)}, u32[]{:S(2)}) copy-start(bf16[1024,256]{1,0:T(8,128)(2,1)} %param.12) | copy-start | bytes 1572868
Sparse Core Ops, SparseCore 0:
  11.2 109.4 all-gather.1
  373.7 100.6 all-reduce.1
  570.8 77.2 reduce-scatter.1
where the time goes:
time: 662 us; the launch traced here: 655 us
  waiting for transfers between devices  189 us (29%)
  local copies, waits for them, and re-layouts  182 us (27%)
  blocking collectives  121 us (18%)
  matrix products  112 us (17%)
  other arithmetic  25.8 us (4%)
  between operations  13.8 us (2%)
  loops' own time  10.1 us (2%)
    gather x1, local copies, waits for them, and re-layouts, local(): fetched = jnp.take(centre_table, list_ids, axis=0)  150 us
    psum x1, blocking collectives, local(): code_sums, counts = lax.psum((code_sums, counts), 'rows')  121 us
    all_gather x1, waiting for transfers between devices, local(): lax.all_gather(centroids, ('rows', 'sub'), axis=0, tiled=True)  111 us
    reduce_scatter x1, waiting for transfers between devices, local(): lax.psum_scatter(jnp.dot(residual.T, rebuilt, preferred_element_type=jnp....  77.4 us
    dot_general x8, matrix products, accumulate(): jnp.einsum('mrk,rmd->mkd', onehot, piece_block, preferred_element_type=jn...  46.9 us
    dot_general x8, matrix products, rebuild_block(): jnp.einsum('mrk,mkd->rmd', onehot, book_rounded, preferred_element_type=j...  31.9 us
    reduce_sum x8, other arithmetic, accumulate(): counts = counts + jnp.sum(onehot, axis=1, dtype=jnp.float32)  22.5 us
    dot_general x1, matrix products, local(): jnp.dot(residual.T, rebuilt, preferred_element_type=jnp.float32) / KS  17.8 us
  transfers between devices with their start and end apart: 3, of which 2 were waited for; matrix products, arithmetic and copies ran while one was open for 0% of the time, Pallas kernels for 0%

commit v1 on v0

v1 whole, which is shorter than its diff:
```python
import jax
import jax.numpy as jnp
from jax import lax
from jax.experimental import pallas as pl
from jax.experimental.pallas import tpu as pltpu
from jax.sharding import PartitionSpec as P

KS = 256
MIB = 2**20
MESH = pl.DeviceIdType.MESH
ROWS, SUBS = 32, 4


def load_table(place, mine_hbm, other_hbm, tab, sem):
    half = mine_hbm.shape[0]
    first = pltpu.make_async_copy(mine_hbm, tab.at[pl.ds(place[1] * half, half)], sem.at[0])
    second = pltpu.make_async_copy(
        other_hbm, tab.at[pl.ds((1 - place[1]) * half, half)], sem.at[1]
    )
    first.start()
    second.start()
    first.wait()
    second.wait()


def gather_rows(ids, base, tab, got, unroll=32):
    def body(i, carry):
        at = [ids[base + i * unroll + j] for j in range(unroll)]
        rows = [tab[at[j]] for j in range(unroll)]
        for j in range(unroll):
            got[i * unroll + j] = rows[j]
        return carry

    lax.fori_loop(0, got.shape[0] // unroll, body, 0)


def sums_kernel(ids, place, vr, codes, mine_hbm, other_hbm, part, tab, got, acc, sem):
    step = pl.program_id(0)
    rows = got.shape[0]

    @pl.when(step == 0)
    def _():
        load_table(place, mine_hbm, other_hbm, tab, sem)
        acc[...] = jnp.zeros_like(acc)

    gather_rows(ids, step * rows, tab, got)
    fetched = got[...].reshape(rows, 256).astype(jnp.float32)
    rotated = vr[...] - fetched
    turned = [rotated[:, h * 128:(h + 1) * 128].T.astype(jnp.bfloat16) for h in range(2)]
    subs = codes.shape[0]
    high = lax.broadcasted_iota(jnp.int32, (64, rows), 0)
    low = lax.broadcasted_iota(jnp.int32, (4, rows), 0)
    for grp in range(subs // 4):
        a, b, n = [], [], []
        for m in range(4 * grp, 4 * grp + 4):
            code = codes[m:m + 1, :]
            a.append((high == (code & 63)).astype(jnp.bfloat16))
            mine = (low == (code >> 6)).astype(jnp.bfloat16)
            piece = turned[m // 8][(m % 8) * 16:(m % 8 + 1) * 16, :]
            for l in range(4):
                b.append(piece * mine[l:l + 1, :])
            n.append(mine)
        left = jnp.concatenate(b + n, axis=0)
        right = jnp.concatenate(a, axis=0)
        acc[grp] += lax.dot_general(
            left, right, (((1,), (1,)), ((), ())), preferred_element_type=jnp.float32
        )

    @pl.when(step == pl.num_programs(0) - 1)
    def _():
        lane = lax.broadcasted_iota(jnp.int32, (1, 128), 1)
        for grp in range(subs // 4):
            for pair in range(2):
                cols = slice(pair * 128, pair * 128 + 128)
                m = 2 * pair
                even = acc[grp, m * 64:(m + 1) * 64, cols]
                odd = acc[grp, (m + 1) * 64:(m + 2) * 64, cols]
                both = jnp.where(lane < 64, even, odd)
                even = acc[grp, 256 + m * 4:256 + m * 4 + 4, cols]
                odd = acc[grp, 256 + m * 4 + 4:256 + m * 4 + 8, cols]
                count = jnp.where(lane < 64, even, odd)
                for l in range(4):
                    at = (2 * grp + pair) * 4 + l
                    part[at, :16, :] = both[l * 16:(l + 1) * 16, :]
                    part[at, 16:, :] = jnp.broadcast_to(count[l:l + 1, :], (8, 128))


def sums_call(ids, place, vr, codes, mine, other):
    rows, width = vr.shape
    subs = codes.shape[0]
    lists = 2 * mine.shape[0]
    tile = 1024
    return pl.pallas_call(
        sums_kernel,
        out_shape=jax.ShapeDtypeStruct((ROWS, 24, 128), jnp.float32),
        grid_spec=pltpu.PrefetchScalarGridSpec(
            num_scalar_prefetch=2,
            grid=(rows // tile,),
            in_specs=[
                pl.BlockSpec((tile, width), lambda i, s, p: (i, 0)),
                pl.BlockSpec((subs, tile), lambda i, s, p: (0, i)),
                pl.BlockSpec(memory_space=pl.ANY),
                pl.BlockSpec(memory_space=pl.ANY),
            ],
            out_specs=pl.BlockSpec((ROWS, 24, 128), lambda i, s, p: (0, 0, 0)),
            scratch_shapes=[
                pltpu.VMEM((lists, 2, 128), jnp.bfloat16),
                pltpu.VMEM((tile, 2, 128), jnp.bfloat16),
                pltpu.VMEM((subs // 4, 272, 256), jnp.float32),
                pltpu.SemaphoreType.DMA((2,)),
            ],
        ),
        compiler_params=pltpu.CompilerParams(vmem_limit_bytes=40 * MIB),
        cost_estimate=pl.CostEstimate(flops=4 * 10**9, bytes_accessed=18 * 10**6, transcendentals=0),
        name="code_sums",
    )(ids, place, vr, codes, mine, other)


def books_kernel(part, books, every, got, chunk, rounded, ssem, rsem, tsem, bsem, xsem, ysem):
    row = lax.axis_index("rows")
    sub = lax.axis_index("sub")
    barrier = pltpu.get_barrier_semaphore()

    def greet(p, carry):
        pl.semaphore_signal(
            barrier, inc=1, device_id=(lax.rem(row + p, ROWS), sub), device_id_type=MESH
        )
        return carry

    lax.fori_loop(1, ROWS, greet, 0)
    for p in range(1, SUBS):
        pl.semaphore_signal(
            barrier, inc=1, device_id=(row, lax.rem(sub + p, SUBS)), device_id_type=MESH
        )
    pl.semaphore_wait(barrier, ROWS - 1 + SUBS - 1)

    def scatter(p):
        to = lax.rem(row + p, ROWS)
        return pltpu.make_async_remote_copy(
            src_ref=part.at[to], dst_ref=got.at[row], send_sem=ssem.at[p],
            recv_sem=rsem.at[row], device_id=(to, sub), device_id_type=MESH,
        )

    def arrival(p):
        source = lax.rem(row + p, ROWS)
        return pltpu.make_async_remote_copy(
            src_ref=part.at[source], dst_ref=got.at[source], send_sem=ssem.at[p],
            recv_sem=rsem.at[source], device_id=(source, sub), device_id_type=MESH,
        )

    lax.fori_loop(1, ROWS, lambda p, c: (scatter(p).start(), c)[1], 0)

    def add(p, total):
        arrival(p).wait_recv()
        return total + got[lax.rem(row + p, ROWS)]

    total = lax.fori_loop(1, ROWS, add, part[row])
    mean = total[:16, :] / total[16:17, :]
    chunk[...] = mean
    books[row] = mean

    def spread(p):
        return pltpu.make_async_remote_copy(
            src_ref=chunk, dst_ref=books.at[row], send_sem=tsem.at[p],
            recv_sem=bsem.at[row], device_id=(lax.rem(row + p, ROWS), sub), device_id_type=MESH,
        )

    def landed(p):
        source = lax.rem(row + p, ROWS)
        return pltpu.make_async_remote_copy(
            src_ref=chunk, dst_ref=books.at[source], send_sem=tsem.at[p],
            recv_sem=bsem.at[source], device_id=(source, sub), device_id_type=MESH,
        )

    lax.fori_loop(1, ROWS, lambda p, c: (spread(p).start(), c)[1], 0)
    lax.fori_loop(1, ROWS, lambda p, c: (landed(p).wait_recv(), c)[1], 0)
    rounded[...] = books[...].astype(jnp.bfloat16)
    every[sub] = rounded[...]

    def across(p):
        return pltpu.make_async_remote_copy(
            src_ref=rounded, dst_ref=every.at[sub], send_sem=xsem.at[p],
            recv_sem=ysem.at[sub], device_id=(row, lax.rem(sub + p, SUBS)), device_id_type=MESH,
        )

    def crossed(p):
        source = lax.rem(sub + p, SUBS)
        return pltpu.make_async_remote_copy(
            src_ref=rounded, dst_ref=every.at[source], send_sem=xsem.at[p],
            recv_sem=ysem.at[source], device_id=(row, source), device_id_type=MESH,
        )

    for p in range(1, SUBS):
        across(p).start()
    for p in range(1, SUBS):
        crossed(p).wait_recv()
        across(p).wait_send()

    def sent(p, carry):
        scatter(p).wait_send()
        spread(p).wait_send()
        return carry

    lax.fori_loop(1, ROWS, sent, 0)


def books_call(part):
    vmem = pl.BlockSpec(memory_space=pltpu.VMEM)
    return pl.pallas_call(
        books_kernel,
        out_shape=(
            jax.ShapeDtypeStruct((ROWS, 16, 128), jnp.float32),
            jax.ShapeDtypeStruct((SUBS, ROWS, 16, 128), jnp.bfloat16),
        ),
        in_specs=[vmem],
        out_specs=(vmem, vmem),
        scratch_shapes=[
            pltpu.VMEM((ROWS, 24, 128), jnp.float32),
            pltpu.VMEM((16, 128), jnp.float32),
            pltpu.VMEM((ROWS, 16, 128), jnp.bfloat16),
            pltpu.SemaphoreType.DMA((ROWS,)),
            pltpu.SemaphoreType.DMA((ROWS,)),
            pltpu.SemaphoreType.DMA((ROWS,)),
            pltpu.SemaphoreType.DMA((ROWS,)),
            pltpu.SemaphoreType.DMA((SUBS,)),
            pltpu.SemaphoreType.DMA((SUBS,)),
        ],
        compiler_params=pltpu.CompilerParams(collective_id=1, has_side_effects=True),
        name="books",
    )(part)


def cross_kernel(ids, place, v, codes, every, mine_hbm, other_hbm, out, tab, got, books, rebuilt, acc, sem):
    step = pl.program_id(0)
    rows = got.shape[0]
    groups = codes.shape[0]

    @pl.when(step == 0)
    def _():
        load_table(place, mine_hbm, other_hbm, tab, sem)
        acc[...] = jnp.zeros_like(acc)
        lane = lax.broadcasted_iota(jnp.int32, (1, 128), 1)

        def relay(q, carry):
            for half in range(2):
                low = every[q, 2 * half].astype(jnp.float32)
                up = every[q, 2 * half + 1].astype(jnp.float32)
                books[2 * q, half] = jnp.where(lane < 64, low, pltpu.roll(up, 64, 1))
                books[2 * q + 1, half] = jnp.where(lane < 64, pltpu.roll(low, 64, 1), up)
            return carry

        lax.fori_loop(0, every.shape[0], relay, 0)

    gather_rows(ids, step * rows, tab, got)
    fetched = got[...].reshape(rows, 256).astype(jnp.float32)
    residual = (v[...].astype(jnp.float32) - fetched).T.astype(jnp.bfloat16)

    def space(g, carry):
        for j in range(8):
            m = g * 8 + j
            table = [[books[m, h, d * 8:(d + 1) * 8, :] for d in range(2)] for h in range(2)]
            for t in range(rows // 128):
                cols = slice(t * 128, (t + 1) * 128)
                code = jnp.broadcast_to(codes[g, j:j + 1, cols], (8, 128))
                at = code & 127
                both = []
                for d in range(2):
                    lo = jnp.take_along_axis(table[0][d], at, axis=1)
                    hi = jnp.take_along_axis(table[1][d], at, axis=1)
                    both.append(jnp.where(code >= 128, hi, lo))
                rebuilt[pl.ds(pl.multiple_of(m * 16, 16), 16), cols] = jnp.concatenate(
                    both, axis=0
                ).astype(jnp.bfloat16)
        return carry

    lax.fori_loop(0, groups, space, 0)
    acc[...] += lax.dot_general(
        residual, rebuilt[...], (((1,), (1,)), ((), ())), preferred_element_type=jnp.float32
    )

    @pl.when(step == pl.num_programs(0) - 1)
    def _():
        for r in range(8):
            for s in range(SUBS):
                out[r, s] = (
                    acc[r * 32:(r + 1) * 32, s * 256:(s + 1) * 256] * (1.0 / KS)
                ).astype(jnp.bfloat16)


def cross_call(ids, place, vectors, codes, every, mine, other):
    rows = vectors.shape[0]
    groups = codes.shape[0]
    lists = 2 * mine.shape[0]
    tile = 1024
    return pl.pallas_call(
        cross_kernel,
        out_shape=jax.ShapeDtypeStruct((8, SUBS, 32, 256), jnp.bfloat16),
        grid_spec=pltpu.PrefetchScalarGridSpec(
            num_scalar_prefetch=2,
            grid=(rows // tile,),
            in_specs=[
                pl.BlockSpec((tile, 256), lambda i, s, p: (i, p[0])),
                pl.BlockSpec((groups, 8, tile), lambda i, s, p: (0, 0, i)),
                pl.BlockSpec((groups * 4, 4, 16, 128), lambda i, s, p: (0, 0, 0, 0)),
                pl.BlockSpec(memory_space=pl.ANY),
                pl.BlockSpec(memory_space=pl.ANY),
            ],
            out_specs=pl.BlockSpec((8, SUBS, 32, 256), lambda i, s, p: (0, 0, 0, 0)),
            scratch_shapes=[
                pltpu.VMEM((lists, 2, 128), jnp.bfloat16),
                pltpu.VMEM((tile, 2, 128), jnp.bfloat16),
                pltpu.VMEM((groups * 8, 2, 16, 128), jnp.float32),
                pltpu.VMEM((groups * 128, tile), jnp.bfloat16),
                pltpu.VMEM((256, 1024), jnp.float32),
                pltpu.SemaphoreType.DMA((2,)),
            ],
        ),
        compiler_params=pltpu.CompilerParams(vmem_limit_bytes=40 * MIB),
        cost_estimate=pl.CostEstimate(flops=5 * 10**9, bytes_accessed=18 * 10**6, transcendentals=0),
        name="cross",
    )(ids, place, vectors, codes, every, mine, other)


def spread_kernel(part, out, got, ssem, rsem):
    row = lax.axis_index("rows")
    sub = lax.axis_index("sub")
    block = row // 8
    own = (sub == block).astype(jnp.int32)
    barrier = pltpu.get_barrier_semaphore()

    def greet(p, carry):
        to = lax.rem(row + p, ROWS)

        @pl.when(jnp.logical_or(to != row, sub != block))
        def _():
            pl.semaphore_signal(barrier, inc=1, device_id=(to, block), device_id_type=MESH)

        return carry

    lax.fori_loop(0, ROWS, greet, 0)
    pl.semaphore_wait(barrier, ROWS - own)

    def copy(p):
        r = lax.rem(row + p // SUBS, 8)
        s = lax.rem(sub + p, SUBS)
        to = sub * 8 + r
        return to, s, r

    def send(p, carry):
        to, s, r = copy(p)
        here = jnp.logical_and(to == row, s == sub)

        @pl.when(here)
        def _():
            pltpu.make_async_copy(part.at[r, s], got.at[row], rsem.at[row]).start()

        @pl.when(jnp.logical_not(here))
        def _():
            pltpu.make_async_remote_copy(
                src_ref=part.at[r, s], dst_ref=got.at[row], send_sem=ssem.at[p],
                recv_sem=rsem.at[row], device_id=(to, s), device_id_type=MESH,
            ).start()

        return carry

    lax.fori_loop(0, ROWS, send, 0)

    def add(p, total):
        source = lax.rem(row + p, ROWS)
        pltpu.make_async_copy(part.at[0, 0], got.at[source], rsem.at[source]).wait()
        return total + got[source].astype(jnp.float32)

    out[...] = lax.fori_loop(0, ROWS, add, jnp.zeros(out.shape, jnp.float32))

    def sent(p, carry):
        to, s, r = copy(p)

        @pl.when(jnp.logical_or(to != row, s != sub))
        def _():
            pltpu.make_async_remote_copy(
                src_ref=part.at[r, s], dst_ref=got.at[row], send_sem=ssem.at[p],
                recv_sem=rsem.at[row], device_id=(to, s), device_id_type=MESH,
            ).wait_send()

        return carry

    lax.fori_loop(0, ROWS, sent, 0)


def spread_call(part):
    vmem = pl.BlockSpec(memory_space=pltpu.VMEM)
    return pl.pallas_call(
        spread_kernel,
        out_shape=jax.ShapeDtypeStruct((32, 256), jnp.float32),
        in_specs=[vmem],
        out_specs=vmem,
        scratch_shapes=[
            pltpu.VMEM((ROWS, 32, 256), jnp.bfloat16),
            pltpu.SemaphoreType.DMA((ROWS,)),
            pltpu.SemaphoreType.DMA((ROWS,)),
        ],
        compiler_params=pltpu.CompilerParams(collective_id=2, has_side_effects=True),
        name="cross_sum",
    )(part)


def around(x):
    sub = lax.axis_index("sub")
    parts = [x]
    for p in range(1, SUBS):
        parts.append(lax.ppermute(x, "sub", [((i + p) % SUBS, i) for i in range(SUBS)]))
    stacked = jnp.zeros((SUBS,) + x.shape, x.dtype)
    for p, part in enumerate(parts):
        stacked = lax.dynamic_update_index_in_dim(stacked, part, lax.rem(sub + p, SUBS), 0)
    return stacked


def fetch(block):
    cores = [[2 * i + c for i in range(ROWS // 2)] for c in range(2)]
    mine = lax.all_gather(block, "rows", axis=0, tiled=True, axis_index_groups=cores)
    other = lax.ppermute(mine, "rows", [(i, i ^ 1) for i in range(ROWS)])
    return mine, other


def local(vectors, list_ids, centroids, rotation, codes):
    row = lax.axis_index("rows")
    sub = lax.axis_index("sub")
    place = jnp.stack([sub, lax.rem(row, 2)]).astype(jnp.int32)
    owner = list_ids // 512
    ids = (owner % 2) * 8192 + (owner // 2) * 512 + list_ids % 512
    near = around(centroids).reshape(512, 1024)
    turned = jnp.dot(near, rotation, preferred_element_type=jnp.float32)
    turned = turned.astype(jnp.bfloat16).reshape(512, 2, 128)
    columns = lax.dynamic_slice_in_dim(near, sub * 256, 256, 1).reshape(512, 2, 128)
    turned_tables = fetch(turned)
    column_tables = fetch(columns)
    vr = jnp.dot(vectors, rotation, preferred_element_type=jnp.float32)
    spaces = around(codes.astype(jnp.bfloat16)).astype(jnp.int32).reshape(8, 8, -1)
    part = sums_call(ids, place, vr, codes, *turned_tables)
    books, every = books_call(part)
    every = every.reshape(32, 4, 16, 128)
    partial = cross_call(ids, place, vectors, spaces, every, *column_tables)
    cross_cov = spread_call(partial)
    codebooks = books.reshape(8, 4, 16, 2, 64).transpose(0, 3, 1, 4, 2).reshape(16, 256, 16)
    return codebooks, cross_cov


def solution(mesh):
    placed = (
        P("rows", None),
        P("rows"),
        P(("rows", "sub"), None),
        P(None, "sub"),
        P("sub", "rows"),
    )
    return jax.shard_map(
        local,
        mesh=mesh,
        in_specs=placed,
        out_specs=(P("sub", None, None), P("rows", "sub")),
        check_vma=False,
    )
```

time: 662 us -> 276 us (0.42)
  local copies, waits for them, and re-layouts: 182 us -> 14.1 us
  Pallas kernels: 0 us -> 122 us
  blocking collectives: 121 us -> 0 us
  matrix products: 112 us -> 14.1 us
  waiting for transfers between devices: 189 us -> 98.8 us
  other arithmetic: 25.8 us -> 1.61 us
  loops' own time: 10.1 us -> 0 us
  starting transfers between devices: 0.12 us -> 9.25 us
    gather x1 -> x0, local copies, waits for them, and re-layouts: 150 us -> none  [local(): fetched = jnp.take(centre_table, list_ids, axis=0)]
    pallas_call x0 -> x4, Pallas kernels: none -> 122 us  [the longest x1 51.1 us: cross_call(): pl.pallas_call(cross_kernel, out_shape=jax.ShapeDtypeStruct((8, SUBS, 32,...]
    psum x1 -> x0, blocking collectives: 121 us -> none  [local(): code_sums, counts = lax.psum((code_sums, counts), 'rows')]
    dot_general x18 -> x2, matrix products: 112 us -> 14.1 us  [the longest x1 13.6 us: local(): vr = jnp.dot(vectors, rotation, preferred_element_type=jnp.float32)]
    reduce_scatter x1 -> x0, waiting for transfers between devices: 77.4 us -> none  [local(): lax.psum_scatter(jnp.dot(residual.T, rebuilt, preferred_element_type=jnp....]
    all_gather x1 -> x2, waiting for transfers between devices: 111 us -> 88.3 us  [fetch(): lax.all_gather(block, 'rows', axis=0, tiled=True, axis_index_groups=cores)]
    dynamic_slice x32 -> x1, local copies, waits for them, and re-layouts: 22.9 us -> 0.04 us  [local(): lax.dynamic_slice_in_dim(near, sub * 256, 256, 1).reshape(512, 2, 128)]
    reduce_sum x8 -> x0, other arithmetic: 22.5 us -> none  [accumulate(): counts = counts + jnp.sum(onehot, axis=1, dtype=jnp.float32)]
  transfers between devices with their start and end apart: 3 -> 10, of which waited for: 2 -> 4; matrix products, arithmetic and copies ran while one was open for 0% -> 6% of each run, Pallas kernels for 0% -> 19%
where the time goes in v1:
time: 276 us; the launch traced here: 274 us
  Pallas kernels  122 us (44%)
  waiting for transfers between devices  98.8 us (36%)
  between operations  14.3 us (5%)
  local copies, waits for them, and re-layouts  14.1 us (5%)
  matrix products  14.1 us (5%)
  starting transfers between devices  9.25 us (3%)
    all_gather x2, waiting for transfers between devices, fetch(): lax.all_gather(block, 'rows', axis=0, tiled=True, axis_index_groups=cores)  88.3 us
    pallas_call x1, Pallas kernels, cross_call(): pl.pallas_call(cross_kernel, out_shape=jax.ShapeDtypeStruct((8, SUBS, 32,...  51.1 us
    pallas_call x1, Pallas kernels, books_call(): pl.pallas_call(books_kernel, out_shape=(jax.ShapeDtypeStruct((ROWS, 16, 1...  28.5 us
    pallas_call x1, Pallas kernels, sums_call(): pl.pallas_call(sums_kernel, out_shape=jax.ShapeDtypeStruct((ROWS, 24, 128...  24.6 us
    pallas_call x1, Pallas kernels, spread_call(): pl.pallas_call(spread_kernel, out_shape=jax.ShapeDtypeStruct((32, 256), j...  17.9 us
    dot_general x1, matrix products, local(): vr = jnp.dot(vectors, rotation, preferred_element_type=jnp.float32)  13.6 us
    ppermute x6, waiting for transfers between devices, around(): lax.ppermute(x, 'sub', [((i + p) % SUBS, i) for i in range(SUBS)])  10.6 us
    unnamed x21, local copies, waits for them, and re-layouts  9.42 us
  transfers between devices with their start and end apart: 10, of which 4 were waited for; matrix products, arithmetic and copies ran while one was open for 6% of the time, Pallas kernels for 19%

profile of v1, /device:TPU:7, one launch (start us, length us, event | category | flops | bytes accessed | tf_op | source)
XLA Modules:
  0.0 274.4 jit_solution(10858683750144984399)
XLA Ops:
  7.2 0.6 collective-permute-start
  7.9 0.7 collective-permute-start.1
  8.5 2.0 collective-permute-start.2
  10.5 0.1 broadcast_in_dim.32
  10.6 1.0 bitcast_dynamic-update-slice_fusion.7
  11.6 9.9 %collective-permute-done = bf16[128,1024]{1,0:T(8,128)(2,1)S(1)} collective-permute-done((bf16[128,1024]{1,0:T(8,128)(2,1)}, bf16[128,1024]{1,0:T(8,128)(2,1)S(1)}, u32[]{:S(2)}, u32[]{:S(2)}) %collective-permute-start) | collective-permute-done | bytes 262176 | tf_op jit(solution)/shard_map/ppermute | solution.py:411
  21.6 0.6 collective-permute-done.2
  22.3 0.5 convolution_convert_fusion
  22.8 0.9 copy.9
  23.8 0.8 reshape.34
  24.7 1.5 collective-permute-start.4
  26.2 3.1 %collective-permute-start.5 = (bf16[16,8192]{1,0:T(8,128)(2,1)S(1)}, bf16[16,8192]{1,0:T(8,128)(2,1)S(1)}, u32[]{:S(2)}, u32[]{:S(2)}) collective-permute-start(bf16[16,8192]{1,0:T(8,128)(2,1)S(1)} %get-tuple-element.7), channel_id=1, source_target_pairs={{2,0},{3,1},{0,2},{1,3},{6,4},{7,5},{4,6},{5,7},{10,8},{11,9},{8,1... | collective-permute-start | bytes 786440 | tf_op jit(solution)/shard_map/ppermute | solution.py:411
  29.3 13.6 %fusion.10.vr = f32[8192,256]{1,0:T(8,128)} fusion(bf16[8192,1024]{1,0:T(8,128)(2,1)} %v.1, bf16[1024,256]{1,0:T(8,128)(2,1)S(1)} %copy-done), kind=kOutput, calls=%fused_computation.33 | convolution fusion | flops 4294967296 | bytes 25690112 | tf_op jit(solution)/shard_map/dot_general | solution.py:437
  43.0 35.5 %all-gather.3.cloned.1.call-done.mine_hbm = bf16[8192,2,128]{2,1,0:T(2,128)(2,1)} async-done(((bf16[512,2,128]{2,1,0:T(2,128)(2,1)}), bf16[8192,2,128]{2,1,0:T(2,128)(2,1)}) %all-gather.3.cloned.1.call-update) | async-done | bytes 4194320 | tf_op jit(solution)/shard_map/all_gather | solution.py:420
  78.5 0.7 collective-permute-start.3
  79.2 52.7 %all-gather.5.cloned.1.call-done.mine_hbm = bf16[8192,2,128]{2,1,0:T(2,128)(2,1)} async-done(((bf16[512,2,128]{2,1,0:T(2,128)(2,1)}), bf16[8192,2,128]{2,1,0:T(2,128)(2,1)}) %all-gather.5.cloned.1.call-update) | async-done | bytes 4194320 | tf_op jit(solution)/shard_map/all_gather | solution.py:420
  131.9 0.7 collective-permute-start.7
  132.7 1.1 copy-done.7
  133.8 1.4 convert.1.codes
  135.2 2.2 copy-done.1
  137.4 24.6 %code_sums.1.part = f32[32,24,128]{2,1,0:T(8,128)S(1)} custom-call(s32[8192]{0:T(1024)S(1)} %fusion.2.ids, s32[2]{0:T(128)S(1)} %pad_add_fusion.place, f32[8192,256]{1,0:T(8,128)} %fusion.10.vr, s32[16,8192]{1,0:T(8,128)S(1)} %copy-done.4, bf16[8192,2,128]{2,1,0:T(2,128)(2,1)S(1)} %copy-done.1, bf16[8192,2,128]{2,1,0:T(2,128)(2,1)} %collective-permute-done.3.other_hbm), custom_call_target="tpu_custom_call" | custom-call | flops 4000000000 | bytes 18000000 | tf_op jit(solution)/shard_map/code_sums/pallas_call | solution.py:93
  162.1 0.8 copy-done.5
  162.8 28.5 %books.1 = (f32[32,16,128]{2,1,0:T(8,128)}, bf16[4,32,16,128]{3,2,1,0:T(8,128)(2,1)}) custom-call(f32[32,24,128]{2,1,0:T(8,128)} %copy-done.5), custom_call_target="tpu_custom_call" | custom-call | tf_op jit(solution)/shard_map/books/pallas_call | solution.py:209
  191.4 2.2 copy-done.2
  193.6 1.0 copy-done.6
  194.6 51.1 %cross.1.part = bf16[8,4,32,256]{3,2,1,0:T(8,128)(2,1)S(1)} custom-call(s32[8192]{0:T(1024)S(1)} %fusion.2.ids, s32[2]{0:T(128)S(1)} %pad_add_fusion.place, bf16[8192,1024]{1,0:T(8,128)(2,1)} %v.1, s32[8,8,8192]{2,1,0:T(8,128)S(1)} %convert.1.codes, bf16[32,4,16,128]{3,2,1,0:T(8,128)(2,1)S(1)} %bitcast.30, bf16[8192,2,128]{2,1,0:T(2,128)(2,1)S(1)} %copy-done.2, ...), custom_call_target="tpu_custom_call" | custom-call | flops 5000000000 | bytes 18000000 | tf_op jit(solution)/shard_map/cross/pallas_call | solution.py:295
  245.7 0.8 copy-done.3
  246.5 17.9 %cross_sum.1 = f32[32,256]{1,0:T(8,128)} custom-call(bf16[8,4,32,256]{3,2,1,0:T(8,128)(2,1)} %copy-done.3), custom_call_target="tpu_custom_call" | custom-call | tf_op jit(solution)/shard_map/cross_sum/pallas_call | solution.py:392
  264.4 0.3 reshape.29
  264.7 0.3 copy.10
  265.1 1.0 reshape.30
  266.1 1.4 copy.20
  (36 shorter events, 0.6 us)
Async XLA Ops:
  7.2 15.1 %copy-start = (bf16[1024,256]{1,0:T(8,128)(2,1)S(1)}, bf16[1024,256]{1,0:T(8,128)(2,1)}, u32[]{:S(2)}) copy-start(bf16[1024,256]{1,0:T(8,128)(2,1)} %param.8) | copy-start | bytes 1572868
  7.2 17.5 %copy-start.4 = (s32[16,8192]{1,0:T(8,128)S(1)}, s32[16,8192]{1,0:T(8,128)}, u32[]{:S(2)}) copy-start(s32[16,8192]{1,0:T(8,128)} %codes.1) | copy-start | bytes 1572868
  7.2 71.3 %all-gather.3.cloned.1.call-start = ((), (), s32[]{:S(2)}) async-start(), calls=%async_computation | async-start | bytes 4456448 | tf_op jit(solution)/shard_map/all_gather | solution.py:420
  7.2 14.3 %collective-permute-start = (bf16[128,1024]{1,0:T(8,128)(2,1)}, bf16[128,1024]{1,0:T(8,128)(2,1)S(1)}, u32[]{:S(2)}, u32[]{:S(2)}) collective-permute-start(bf16[128,1024]{1,0:T(8,128)(2,1)} %param.7), channel_id=1, source_target_pairs={{1,0},{2,1},{3,2},{0,3},{5,4},{6,5},{7,6},{4,7},{9,8},{10,9},{11,1... | collective-permute-start | bytes 786440 | tf_op jit(solution)/shard_map/ppermute | solution.py:411
  7.9 13.7 %collective-permute-start.1 = (bf16[128,1024]{1,0:T(8,128)(2,1)}, bf16[128,1024]{1,0:T(8,128)(2,1)S(1)}, u32[]{:S(2)}, u32[]{:S(2)}) collective-permute-start(bf16[128,1024]{1,0:T(8,128)(2,1)} %param.7), channel_id=1, source_target_pairs={{2,0},{3,1},{0,2},{1,3},{6,4},{7,5},{4,6},{5,7},{10,8},{11,9},{8,1... | collective-permute-start | bytes 786440 | tf_op jit(solution)/shard_map/ppermute | solution.py:411
  8.5 13.7 %collective-permute-start.2 = (bf16[128,1024]{1,0:T(8,128)(2,1)}, bf16[128,1024]{1,0:T(8,128)(2,1)S(1)}, u32[]{:S(2)}, u32[]{:S(2)}) collective-permute-start(bf16[128,1024]{1,0:T(8,128)(2,1)} %param.7), channel_id=1, source_target_pairs={{3,0},{0,1},{1,2},{2,3},{7,4},{4,5},{5,6},{6,7},{11,8},{8,9},{9,10... | collective-permute-start | bytes 786440 | tf_op jit(solution)/shard_map/ppermute | solution.py:411
  23.7 108.2 %all-gather.5.cloned.1.call-start = ((), (), s32[]{:S(2)}) async-start(), calls=%async_computation.1 | async-start | bytes 4456448 | tf_op jit(solution)/shard_map/all_gather | solution.py:420
  24.7 107.9 %collective-permute-start.4 = (bf16[16,8192]{1,0:T(8,128)(2,1)S(1)}, bf16[16,8192]{1,0:T(8,128)(2,1)S(1)}, u32[]{:S(2)}, u32[]{:S(2)}) collective-permute-start(bf16[16,8192]{1,0:T(8,128)(2,1)S(1)} %get-tuple-element.7), channel_id=1, source_target_pairs={{1,0},{2,1},{3,2},{0,3},{5,4},{6,5},{7,6},{4,7},{9,8},{10,9},{11,1... | collective-permute-start | bytes 786440 | tf_op jit(solution)/shard_map/ppermute | solution.py:411
  26.2 106.4 %collective-permute-start.5 = (bf16[16,8192]{1,0:T(8,128)(2,1)S(1)}, bf16[16,8192]{1,0:T(8,128)(2,1)S(1)}, u32[]{:S(2)}, u32[]{:S(2)}) collective-permute-start(bf16[16,8192]{1,0:T(8,128)(2,1)S(1)} %get-tuple-element.7), channel_id=1, source_target_pairs={{2,0},{3,1},{0,2},{1,3},{6,4},{7,5},{4,6},{5,7},{10,8},{11,9},{8,1... | collective-permute-start | bytes 786440 | tf_op jit(solution)/shard_map/ppermute | solution.py:411
  29.3 103.4 %collective-permute-start.6 = (bf16[16,8192]{1,0:T(8,128)(2,1)S(1)}, bf16[16,8192]{1,0:T(8,128)(2,1)S(1)}, u32[]{:S(2)}, u32[]{:S(2)}) collective-permute-start(bf16[16,8192]{1,0:T(8,128)(2,1)S(1)} %get-tuple-element.7), channel_id=1, source_target_pairs={{3,0},{0,1},{1,2},{2,3},{7,4},{4,5},{5,6},{6,7},{11,8},{8,9},{9,10... | collective-permute-start | bytes 786440 | tf_op jit(solution)/shard_map/ppermute | solution.py:411
  29.3 13.6 %copy-start.9 = (s32[8192]{0:T(1024)S(1)}, s32[8192]{0:T(1024)}, u32[]{:S(2)}) copy-start(s32[8192]{0:T(1024)} %param.6) | copy-start | bytes 98308
  78.5 56.7 %collective-permute-start.3 = (bf16[8192,2,128]{2,1,0:T(2,128)(2,1)}, bf16[8192,2,128]{2,1,0:T(2,128)(2,1)}, u32[]{:S(2)}, u32[]{:S(2)}) collective-permute-start(bf16[8192,2,128]{2,1,0:T(2,128)(2,1)} %all-gather.3.cloned.1.call-done.mine_hbm), channel_id=1, source_target_pairs={{0,4},{4,0},{8,12},{12,8},{16,20},{20,16},{24,28},{28,24},{32,36},... | collective-permute-start | bytes 12582920 | tf_op jit(solution)/shard_map/ppermute | solution.py:421
  131.9 59.5 %collective-permute-start.7 = (bf16[8192,2,128]{2,1,0:T(2,128)(2,1)}, bf16[8192,2,128]{2,1,0:T(2,128)(2,1)}, u32[]{:S(2)}, u32[]{:S(2)}) collective-permute-start(bf16[8192,2,128]{2,1,0:T(2,128)(2,1)} %all-gather.5.cloned.1.call-done.mine_hbm), channel_id=1, source_target_pairs={{0,4},{4,0},{8,12},{12,8},{16,20},{20,16},{24,28},{28,24},{32,36},... | collective-permute-start | bytes 12582920 | tf_op jit(solution)/shard_map/ppermute | solution.py:421
  132.7 1.1 copy-start.7
  135.2 2.2 copy-start.1
  162.0 0.8 copy-start.5
  191.4 2.2 copy-start.2
  193.6 1.0 copy-start.6
  194.6 69.8 %copy-start.8 = (f32[32,16,128]{2,1,0:T(8,128)S(1)}, f32[32,16,128]{2,1,0:T(8,128)}, u32[]{:S(2)}) copy-start(f32[32,16,128]{2,1,0:T(8,128)} %get-tuple-element.4) | copy-start | bytes 786436
  245.7 0.8 copy-start.3
Sparse Core Ops, SparseCore 0:
  23.8 54.6 all-gather.2
  80.6 51.2 all-gather.4

commit v2 on v1

--- a/solution.py
+++ b/solution.py
@@ -11,16 +11,10 @@
 ROWS, SUBS = 32, 4
 
 
-def load_table(place, mine_hbm, other_hbm, tab, sem):
-    half = mine_hbm.shape[0]
-    first = pltpu.make_async_copy(mine_hbm, tab.at[pl.ds(place[1] * half, half)], sem.at[0])
-    second = pltpu.make_async_copy(
-        other_hbm, tab.at[pl.ds((1 - place[1]) * half, half)], sem.at[1]
-    )
-    first.start()
-    second.start()
-    first.wait()
-    second.wait()
+def load_table(table_hbm, tab, sem):
+    copy = pltpu.make_async_copy(table_hbm, tab, sem)
+    copy.start()
+    copy.wait()
 
 
 def gather_rows(ids, base, tab, got, unroll=32):
@@ -34,18 +28,18 @@
     lax.fori_loop(0, got.shape[0] // unroll, body, 0)
 
 
-def sums_kernel(ids, place, vr, codes, mine_hbm, other_hbm, part, tab, got, acc, sem):
+def sums_kernel(ids, v, rot, codes, table_hbm, part, tab, got, acc, sem):
     step = pl.program_id(0)
     rows = got.shape[0]
 
     @pl.when(step == 0)
     def _():
-        load_table(place, mine_hbm, other_hbm, tab, sem)
+        load_table(table_hbm, tab, sem)
         acc[...] = jnp.zeros_like(acc)
 
     gather_rows(ids, step * rows, tab, got)
     fetched = got[...].reshape(rows, 256).astype(jnp.float32)
-    rotated = vr[...] - fetched
+    rotated = jnp.dot(v[...], rot[...], preferred_element_type=jnp.float32) - fetched
     turned = [rotated[:, h * 128:(h + 1) * 128].T.astype(jnp.bfloat16) for h in range(2)]
     subs = codes.shape[0]
     high = lax.broadcasted_iota(jnp.int32, (64, rows), 0)
@@ -85,35 +79,35 @@
                     part[at, 16:, :] = jnp.broadcast_to(count[l:l + 1, :], (8, 128))
 
 
-def sums_call(ids, place, vr, codes, mine, other):
-    rows, width = vr.shape
+def sums_call(ids, vectors, rotation, codes, table):
+    rows, width = vectors.shape
     subs = codes.shape[0]
-    lists = 2 * mine.shape[0]
+    lists = table.shape[0]
     tile = 1024
     return pl.pallas_call(
         sums_kernel,
         out_shape=jax.ShapeDtypeStruct((ROWS, 24, 128), jnp.float32),
         grid_spec=pltpu.PrefetchScalarGridSpec(
-            num_scalar_prefetch=2,
+            num_scalar_prefetch=1,
             grid=(rows // tile,),
             in_specs=[
-                pl.BlockSpec((tile, width), lambda i, s, p: (i, 0)),
-                pl.BlockSpec((subs, tile), lambda i, s, p: (0, i)),
-                pl.BlockSpec(memory_space=pl.ANY),
+                pl.BlockSpec((tile, width), lambda i, s: (i, 0)),
+                pl.BlockSpec(rotation.shape, lambda i, s: (0, 0)),
+                pl.BlockSpec((subs, tile), lambda i, s: (0, i)),
                 pl.BlockSpec(memory_space=pl.ANY),
             ],
-            out_specs=pl.BlockSpec((ROWS, 24, 128), lambda i, s, p: (0, 0, 0)),
+            out_specs=pl.BlockSpec((ROWS, 24, 128), lambda i, s: (0, 0, 0)),
             scratch_shapes=[
                 pltpu.VMEM((lists, 2, 128), jnp.bfloat16),
                 pltpu.VMEM((tile, 2, 128), jnp.bfloat16),
                 pltpu.VMEM((subs // 4, 272, 256), jnp.float32),
-                pltpu.SemaphoreType.DMA((2,)),
+                pltpu.SemaphoreType.DMA,
             ],
         ),
         compiler_params=pltpu.CompilerParams(vmem_limit_bytes=40 * MIB),
-        cost_estimate=pl.CostEstimate(flops=4 * 10**9, bytes_accessed=18 * 10**6, transcendentals=0),
+        cost_estimate=pl.CostEstimate(flops=35 * 10**9, bytes_accessed=18 * 10**6, transcendentals=0),
         name="code_sums",
-    )(ids, place, vr, codes, mine, other)
+    )(ids, vectors, rotation, codes, table)
 
 
 def books_kernel(part, books, every, got, chunk, rounded, ssem, rsem, tsem, bsem, xsem, ysem):
@@ -226,18 +220,19 @@
             pltpu.SemaphoreType.DMA((SUBS,)),
         ],
         compiler_params=pltpu.CompilerParams(collective_id=1, has_side_effects=True),
+        cost_estimate=pl.CostEstimate(flops=20 * 10**9, bytes_accessed=10**6, transcendentals=0),
         name="books",
     )(part)
 
 
-def cross_kernel(ids, place, v, codes, every, mine_hbm, other_hbm, out, tab, got, books, rebuilt, acc, sem):
+def cross_kernel(ids, place, v, codes, every, table_hbm, out, tab, got, books, rebuilt, acc, sem):
     step = pl.program_id(0)
     rows = got.shape[0]
     groups = codes.shape[0]
 
     @pl.when(step == 0)
     def _():
-        load_table(place, mine_hbm, other_hbm, tab, sem)
+        load_table(table_hbm, tab, sem)
         acc[...] = jnp.zeros_like(acc)
         lane = lax.broadcasted_iota(jnp.int32, (1, 128), 1)
 
@@ -287,10 +282,10 @@
                 ).astype(jnp.bfloat16)
 
 
-def cross_call(ids, place, vectors, codes, every, mine, other):
+def cross_call(ids, place, vectors, codes, every, table):
     rows = vectors.shape[0]
     groups = codes.shape[0]
-    lists = 2 * mine.shape[0]
+    lists = table.shape[0]
     tile = 1024
     return pl.pallas_call(
         cross_kernel,
@@ -303,7 +298,6 @@
                 pl.BlockSpec((groups, 8, tile), lambda i, s, p: (0, 0, i)),
                 pl.BlockSpec((groups * 4, 4, 16, 128), lambda i, s, p: (0, 0, 0, 0)),
                 pl.BlockSpec(memory_space=pl.ANY),
-                pl.BlockSpec(memory_space=pl.ANY),
             ],
             out_specs=pl.BlockSpec((8, SUBS, 32, 256), lambda i, s, p: (0, 0, 0, 0)),
             scratch_shapes=[
@@ -312,13 +306,13 @@
                 pltpu.VMEM((groups * 8, 2, 16, 128), jnp.float32),
                 pltpu.VMEM((groups * 128, tile), jnp.bfloat16),
                 pltpu.VMEM((256, 1024), jnp.float32),
-                pltpu.SemaphoreType.DMA((2,)),
+                pltpu.SemaphoreType.DMA,
             ],
         ),
         compiler_params=pltpu.CompilerParams(vmem_limit_bytes=40 * MIB),
-        cost_estimate=pl.CostEstimate(flops=5 * 10**9, bytes_accessed=18 * 10**6, transcendentals=0),
+        cost_estimate=pl.CostEstimate(flops=50 * 10**9, bytes_accessed=18 * 10**6, transcendentals=0),
         name="cross",
-    )(ids, place, vectors, codes, every, mine, other)
+    )(ids, place, vectors, codes, every, table)
 
 
 def spread_kernel(part, out, got, ssem, rsem):
@@ -415,31 +409,199 @@
     return stacked
 
 
-def fetch(block):
-    cores = [[2 * i + c for i in range(ROWS // 2)] for c in range(2)]
-    mine = lax.all_gather(block, "rows", axis=0, tiled=True, axis_index_groups=cores)
-    other = lax.ppermute(mine, "rows", [(i, i ^ 1) for i in range(ROWS)])
-    return mine, other
+ROUNDS = ((0, 1), (1, 3), (3, 4))
+
+
+def table_kernel(c, rot, table, columns, near, stage, ssem, rsem, xssem, xrsem, lsem):
+    row = lax.axis_index("rows")
+    sub = lax.axis_index("sub")
+    core = lax.rem(row, 2)
+    z = lax.rem(row // 2, 4)
+    y = row // 8
+
+    def up(i):
+        return lax.rem(i + 1, 4)
+
+    def down(i):
+        return lax.rem(i + 3, 4)
+
+    def device(at_y, at_z):
+        return ((at_y * 4 + at_z) * 2 + core, sub)
+
+    beside = (row + 1 - 2 * core, sub)
+    after = {0: (device(up(y), z), device(down(y), z)), 1: (device(y, up(z)), device(y, down(z)))}
+    across = ((row, up(sub)), (row, down(sub)))
+
+    barrier = pltpu.get_barrier_semaphore()
+    for peer in after[0] + after[1] + across + (beside,):
+        pl.semaphore_signal(barrier, inc=1, device_id=peer, device_id_type=MESH)
+    pl.semaphore_wait(barrier, 7)
+
+    def remote(src, dst, send, recv, to):
+        return pltpu.make_async_remote_copy(
+            src_ref=src, dst_ref=dst, send_sem=send, recv_sem=recv,
+            device_id=to, device_id_type=MESH,
+        )
+
+    def exchange(k):
+        if k < 2:
+            return remote(c, near.at[1 - k], xssem.at[k], xrsem.at[k], across[k])
+        half = pl.ds((k - 2) * 64, 64)
+        return remote(near.at[3 - k, half], near.at[2, half], xssem.at[k], xrsem.at[k], across[k - 2])
+
+    exchange(0).start()
+    exchange(1).start()
+
+    def project(q, block):
+        value = jnp.dot(block, rot[...], preferred_element_type=jnp.float32)
+        value = value.astype(jnp.bfloat16).reshape(2, 64, 2, 128)
+        stage[q] = value
+
+    def hop(rnd, h, phase, k):
+        first, last = ROUNDS[rnd]
+        qs = pl.ds(first, last - first)
+        u, w = (y, z) if h == 0 else (z, y)
+        to = after[h if phase == 0 else 1 - h][k % 2]
+        at = ((rnd * 2 + h) * 2 + phase) * 4 + k
+        mine = table.at[core, h]
+        part = pl.ds(0, 32) if k == 2 else pl.ds(32, 32)
+        if phase == 0:
+            dst = mine.at[w, u, qs]
+            if k < 2:
+                src = stage.at[qs, h]
+            else:
+                src = dst = mine.at[w, down(u) if k == 2 else up(u), qs, part]
+        elif k < 2:
+            src = dst = mine.at[w, :, qs]
+        else:
+            src = dst = mine.at[down(w) if k == 2 else up(w), :, qs, part]
+        return remote(src, dst, ssem.at[at], rsem.at[at], to)
+
+    def keep(rnd, h):
+        first, last = ROUNDS[rnd]
+        qs = pl.ds(first, last - first)
+        u, w = (y, z) if h == 0 else (z, y)
+        return pltpu.make_async_copy(
+            stage.at[qs, h], table.at[core, h, w, u, qs], lsem.at[rnd * 2 + h]
+        )
+
+    def over(rnd, h):
+        first, last = ROUNDS[rnd]
+        part = table.at[core, h, :, :, pl.ds(first, last - first)]
+        at = 48 + rnd * 2 + h
+        return remote(part, part, ssem.at[at], rsem.at[at], beside)
+
+    def start(rnd, phase, forward):
+        for k in (2, 3) if forward else (0, 1):
+            for h in range(2):
+                if forward:
+                    hop(rnd, h, phase, k - 2).wait_recv()
+                hop(rnd, h, phase, k).start()
+
+    def arrived(rnd, phase):
+        for h in range(2):
+            for k in (2, 3):
+                hop(rnd, h, phase, k).wait_recv()
+
+    def begin(rnd):
+        for h in range(2):
+            keep(rnd, h).start()
+        start(rnd, 0, False)
+
+    def second(rnd):
+        arrived(rnd, 0)
+        for h in range(2):
+            keep(rnd, h).wait()
+        start(rnd, 1, False)
+
+    def finish(rnd):
+        arrived(rnd, 1)
+        for h in range(2):
+            over(rnd, h).start()
+
+    project(0, c[...])
+    begin(0)
+    for k in range(2):
+        exchange(k).wait_recv()
+        exchange(k + 2).start()
+    start(0, 0, True)
+    project(1, near[0])
+    project(2, near[1])
+    begin(1)
+    second(0)
+    exchange(2).wait_recv()
+    exchange(3).wait_recv()
+    project(3, near[2])
+    begin(2)
+    start(1, 0, True)
+    second(1)
+    start(2, 0, True)
+    second(2)
+    start(0, 1, True)
+    first_column = pl.multiple_of(sub * 256, 256)
+    for q in range(4):
+        block = c[:, pl.ds(first_column, 256)] if q == 0 else near[q - 1, :, pl.ds(first_column, 256)]
+        columns[q] = block.reshape(128, 2, 128)
+    finish(0)
+    start(1, 1, True)
+    finish(1)
+    start(2, 1, True)
+    finish(2)
+    for rnd in range(3):
+        for h in range(2):
+            over(rnd, h).wait()
+            for phase in range(2):
+                for k in range(4):
+                    hop(rnd, h, phase, k).wait_send()
+    for k in range(4):
+        exchange(k).wait_send()
+
+
+def table_call(centroids, rotation):
+    vmem = pl.BlockSpec(memory_space=pltpu.VMEM)
+    dma = pltpu.SemaphoreType.DMA
+    return pl.pallas_call(
+        table_kernel,
+        out_shape=(
+            jax.ShapeDtypeStruct((2, 2, 4, 4, 4, 64, 2, 128), jnp.bfloat16),
+            jax.ShapeDtypeStruct((4, 128, 2, 128), jnp.bfloat16),
+        ),
+        in_specs=[vmem, vmem],
+        out_specs=(pl.BlockSpec(memory_space=pl.ANY), vmem),
+        scratch_shapes=[
+            pltpu.VMEM((3, 128, 1024), jnp.bfloat16),
+            pltpu.VMEM((4, 2, 64, 2, 128), jnp.bfloat16),
+            dma((54,)),
+            dma((54,)),
+            dma((4,)),
+            dma((4,)),
+            dma((6,)),
+        ],
+        compiler_params=pltpu.CompilerParams(collective_id=3, has_side_effects=True),
+        cost_estimate=pl.CostEstimate(flops=10**9, bytes_accessed=10**8, transcendentals=0),
+        name="table",
+    )(centroids, rotation)
 
 
 def local(vectors, list_ids, centroids, rotation, codes):
     row = lax.axis_index("rows")
     sub = lax.axis_index("sub")
     place = jnp.stack([sub, lax.rem(row, 2)]).astype(jnp.int32)
-    owner = list_ids // 512
-    ids = (owner % 2) * 8192 + (owner // 2) * 512 + list_ids % 512
-    near = around(centroids).reshape(512, 1024)
-    turned = jnp.dot(near, rotation, preferred_element_type=jnp.float32)
-    turned = turned.astype(jnp.bfloat16).reshape(512, 2, 128)
-    columns = lax.dynamic_slice_in_dim(near, sub * 256, 256, 1).reshape(512, 2, 128)
-    turned_tables = fetch(turned)
-    column_tables = fetch(columns)
-    vr = jnp.dot(vectors, rotation, preferred_element_type=jnp.float32)
+    table, columns = table_call(centroids, rotation)
+    column_table = lax.all_gather(columns, "rows", axis=0, tiled=True)
     spaces = around(codes.astype(jnp.bfloat16)).astype(jnp.int32).reshape(8, 8, -1)
-    part = sums_call(ids, place, vr, codes, *turned_tables)
+    owner, inner = list_ids // 128, list_ids % 128
+    at_row, at_sub = owner // 4, owner % 4
+    near = jnp.array([0, 1, 3, 2], jnp.int32)[(at_sub - sub + 4) % 4]
+    at_y, at_z, at_core = at_row // 8, (at_row // 2) % 4, at_row % 2
+    half = inner // 64
+    block = jnp.where(half == 0, at_z * 4 + at_y, at_y * 4 + at_z)
+    ids = (((at_core * 2 + half) * 16 + block) * 4 + near) * 64 + inner % 64
+    column_ids = (at_row * 4 + near) * 128 + inner
+    part = sums_call(ids, vectors, rotation, codes, table.reshape(-1, 2, 128))
     books, every = books_call(part)
     every = every.reshape(32, 4, 16, 128)
-    partial = cross_call(ids, place, vectors, spaces, every, *column_tables)
+    partial = cross_call(column_ids, place, vectors, spaces, every, column_table.reshape(-1, 2, 128))
     cross_cov = spread_call(partial)
     codebooks = books.reshape(8, 4, 16, 2, 64).transpose(0, 3, 1, 4, 2).reshape(16, 256, 16)
     return codebooks, cross_cov

time: 276 us -> 229 us (0.83)
  waiting for transfers between devices: 98.8 us -> 0.05 us
  Pallas kernels: 122 us -> 179 us
  matrix products: 14.1 us -> 0 us
  local copies, waits for them, and re-layouts: 14.1 us -> 27.4 us
  starting transfers between devices: 9.25 us -> 5.05 us
    all_gather x2 -> x1, waiting for transfers between devices: 88.3 us -> 0.02 us  [local(): column_table = lax.all_gather(columns, 'rows', axis=0, tiled=True)]
    pallas_call x0 -> x1, Pallas kernels: none -> 50.9 us  [table_call(): pl.pallas_call(table_kernel, out_shape=(jax.ShapeDtypeStruct((2, 2, 4, 4,...]
    all_gather x0 -> x1, local copies, waits for them, and re-layouts: none -> 14.4 us  [local(): column_table = lax.all_gather(columns, 'rows', axis=0, tiled=True)]
    dot_general x2 -> x0, matrix products: 14.1 us -> none  [the longest x1 13.6 us: local(): vr = jnp.dot(vectors, rotation, preferred_element_type=jnp.float32)]
    ppermute x6 -> x3, waiting for transfers between devices: 10.6 us -> 0.01 us  [around(): lax.ppermute(x, 'sub', [((i + p) % SUBS, i) for i in range(SUBS)])]
    pallas_call x1, Pallas kernels: 24.6 us -> 32.3 us  [sums_call(): pl.pallas_call(sums_kernel, out_shape=jax.ShapeDtypeStruct((ROWS, 24, 128...]
    ppermute x6 -> x3, starting transfers between devices: 7.82 us -> 5.02 us  [around(): lax.ppermute(x, 'sub', [((i + p) % SUBS, i) for i in range(SUBS)])]
    unnamed x21 -> x13, local copies, waits for them, and re-layouts: 9.42 us -> 8.48 us
  transfers between devices with their start and end apart: 10 -> 4, of which waited for: 4 -> 0; matrix products, arithmetic and copies ran while one was open for 6% -> 2% of each run, Pallas kernels for 19% -> 26%
where the time goes in v2:
time: 229 us; the launch traced here: 228 us
  Pallas kernels  179 us (78%)
  local copies, waits for them, and re-layouts  27.4 us (12%)
  between operations  14.2 us (6%)
  starting transfers between devices  5.05 us (2%)
  other arithmetic  2.31 us (1%)
    pallas_call x1, Pallas kernels, table_call(): pl.pallas_call(table_kernel, out_shape=(jax.ShapeDtypeStruct((2, 2, 4, 4,...  50.9 us
    pallas_call x1, Pallas kernels, cross_call(): pl.pallas_call(cross_kernel, out_shape=jax.ShapeDtypeStruct((8, SUBS, 32,...  49.2 us
    pallas_call x1, Pallas kernels, sums_call(): pl.pallas_call(sums_kernel, out_shape=jax.ShapeDtypeStruct((ROWS, 24, 128...  32.3 us
    pallas_call x1, Pallas kernels, books_call(): pl.pallas_call(books_kernel, out_shape=(jax.ShapeDtypeStruct((ROWS, 16, 1...  27.9 us
    pallas_call x1, Pallas kernels, spread_call(): pl.pallas_call(spread_kernel, out_shape=jax.ShapeDtypeStruct((32, 256), j...  18.3 us
    all_gather x1, local copies, waits for them, and re-layouts, local(): column_table = lax.all_gather(columns, 'rows', axis=0, tiled=True)  14.4 us
    unnamed x13, local copies, waits for them, and re-layouts  8.48 us
    ppermute x3, starting transfers between devices, around(): lax.ppermute(x, 'sub', [((i + p) % SUBS, i) for i in range(SUBS)])  5.02 us
  transfers between devices with their start and end apart: 4, of which 0 were waited for; matrix products, arithmetic and copies ran while one was open for 2% of the time, Pallas kernels for 26%

profile of v2, /device:TPU:7, one launch (start us, length us, event | category | flops | bytes accessed | tf_op | source)
XLA Modules:
  0.0 227.7 jit_solution(13452578339351107782)
XLA Ops:
  7.2 0.0 all-gather.2.cloned.1.call-start
  7.2 50.9 %table.1 = (bf16[2,2,4,4,4,64,2,128]{7,6,5,4,3,2,1,0:T(2,128)(2,1)}, bf16[4,128,2,128]{3,2,1,0:T(2,128)(2,1)}) custom-call(bf16[128,1024]{1,0:T(8,128)(2,1)} %c.1, bf16[1024,256]{1,0:T(8,128)(2,1)} %rot.3), custom_call_target="tpu_custom_call" | custom-call | flops 1000000000 | bytes 100000000 | tf_op jit(solution)/shard_map/table/pallas_call | solution.py:563
  58.2 1.7 copy.10
  59.8 0.0 all-gather.2.cloned.1.call-update
  59.9 0.1 broadcast_in_dim.20
  60.0 1.1 bitcast_dynamic-update-slice_fusion.3
  61.0 2.3 %collective-permute-start.1 = (bf16[16,8192]{1,0:T(8,128)(2,1)S(1)}, bf16[16,8192]{1,0:T(8,128)(2,1)S(1)}, u32[]{:S(2)}, u32[]{:S(2)}) collective-permute-start(bf16[16,8192]{1,0:T(8,128)(2,1)S(1)} %get-tuple-element.11), channel_id=1, source_target_pairs={{2,0},{3,1},{0,2},{1,3},{6,4},{7,5},{4,6},{5,7},{10,8},{11,9},{8,1... | collective-permute-start | bytes 786440 | tf_op jit(solution)/shard_map/ppermute | solution.py:405
  63.4 0.0 collective-permute-start
  63.4 2.7 %collective-permute-start.2 = (bf16[16,8192]{1,0:T(8,128)(2,1)S(1)}, bf16[16,8192]{1,0:T(8,128)(2,1)S(1)}, u32[]{:S(2)}, u32[]{:S(2)}) collective-permute-start(bf16[16,8192]{1,0:T(8,128)(2,1)S(1)} %get-tuple-element.11), channel_id=1, source_target_pairs={{3,0},{0,1},{1,2},{2,3},{7,4},{4,5},{5,6},{6,7},{11,8},{8,9},{9,10... | collective-permute-start | bytes 786440 | tf_op jit(solution)/shard_map/ppermute | solution.py:405
  66.1 0.9 multiply_add_fusion
  67.0 0.0 copy-start.1
  67.0 1.1 copy-done.1
  68.1 1.1 copy-done.2
  69.1 3.4 %copy-done.3 = bf16[2,2,4,4,4,64,2,128]{7,6,5,4,3,2,1,0:T(2,128)(2,1)S(1)} copy-done((bf16[2,2,4,4,4,64,2,128]{7,6,5,4,3,2,1,0:T(2,128)(2,1)S(1)}, bf16[2,2,4,4,4,64,2,128]{7,6,5,4,3,2,1,0:T(2,128)(2,1)}, u32[]{:S(2)}) %copy-start.3) | copy-done | bytes 8388632
  72.6 32.3 %code_sums.1.part = f32[32,24,128]{2,1,0:T(8,128)S(1)} custom-call(s32[8192]{0:T(1024)S(1)} %get-tuple-element.13.ids, bf16[8192,1024]{1,0:T(8,128)(2,1)} %v.3, bf16[1024,256]{1,0:T(8,128)(2,1)S(1)} %copy-done.2, s32[16,8192]{1,0:T(8,128)S(1)} %copy-done.1, bf16[16384,2,128]{2,1,0:T(2,128)(2,1)S(1)} %bitcast.19), custom_call_target="tpu_custom_call" | custom-call | flops 35000000512 | bytes 18000000 | tf_op jit(solution)/shard_map/code_sums/pallas_call | solution.py:87
  104.9 0.8 copy-done.5
  105.6 27.9 %books.1 = (f32[32,16,128]{2,1,0:T(8,128)}, bf16[4,32,16,128]{3,2,1,0:T(8,128)(2,1)}) custom-call(f32[32,24,128]{2,1,0:T(8,128)} %copy-done.5), custom_call_target="tpu_custom_call" | custom-call | flops 20000000000 | bytes 1000000 | tf_op jit(solution)/shard_map/books/pallas_call | solution.py:203
  133.6 1.3 reshape.25
  134.8 0.3 copy.9
  135.2 1.0 reshape.26
  136.2 0.1 pad_add_fusion.place
  136.3 0.0 collective-permute-done
  136.3 0.0 collective-permute-done.1
  136.4 0.0 collective-permute-done.2
  136.4 0.2 convert.1.codes
  136.6 0.0 copy-start.4
  136.6 0.0 all-gather.2.cloned.1.call-done
  136.7 14.4 %copy.11 = bf16[128,128,2,128]{3,2,1,0:T(2,128)(2,1)S(1)} copy(bf16[128,128,2,128]{3,1,2,0:T(8,128)(2,1)} %all-gather.2.cloned.1.call-done) | data formatting | bytes 16777216 | tf_op jit(solution)/shard_map/all_gather | solution.py:591
  151.1 49.2 %cross.1.part = bf16[8,4,32,256]{3,2,1,0:T(8,128)(2,1)S(1)} custom-call(s32[8192]{0:T(1024)S(1)} %get-tuple-element.12.ids, s32[2]{0:T(128)S(1)} %pad_add_fusion.place, bf16[8192,1024]{1,0:T(8,128)(2,1)} %v.3, s32[8,8,8192]{2,1,0:T(8,128)S(1)} %convert.1.codes, bf16[32,4,16,128]{3,2,1,0:T(8,128)(2,1)S(1)} %bitcast.20, bf16[16384,2,128]{2,1,0:T(2,128)(2,1)S(1)} %bitcast.18), custom_call_target="tpu_custom_call" | custom-call | flops 49999998976 | bytes 18000000 | tf_op jit(solution)/shard_map/cross/pallas_call | solution.py:290
  200.3 0.8 copy-done
  201.1 18.3 %cross_sum.1 = f32[32,256]{1,0:T(8,128)} custom-call(bf16[8,4,32,256]{3,2,1,0:T(8,128)(2,1)} %copy-done), custom_call_target="tpu_custom_call" | custom-call | tf_op jit(solution)/shard_map/cross_sum/pallas_call | solution.py:386
  219.4 1.4 copy.17
  (8 shorter events, 0.1 us)
Async XLA Ops:
  7.2 129.5 %all-gather.2.cloned.1.call-start = ((), (), s32[]{:S(2)}) async-start(), calls=%async_computation | async-start | bytes 8650752 | tf_op jit(solution)/shard_map/all_gather | solution.py:591
  61.0 75.3 %collective-permute-start.1 = (bf16[16,8192]{1,0:T(8,128)(2,1)S(1)}, bf16[16,8192]{1,0:T(8,128)(2,1)S(1)}, u32[]{:S(2)}, u32[]{:S(2)}) collective-permute-start(bf16[16,8192]{1,0:T(8,128)(2,1)S(1)} %get-tuple-element.11), channel_id=1, source_target_pairs={{2,0},{3,1},{0,2},{1,3},{6,4},{7,5},{4,6},{5,7},{10,8},{11,9},{8,1... | collective-permute-start | bytes 786440 | tf_op jit(solution)/shard_map/ppermute | solution.py:405
  63.4 72.9 %collective-permute-start = (bf16[16,8192]{1,0:T(8,128)(2,1)S(1)}, bf16[16,8192]{1,0:T(8,128)(2,1)S(1)}, u32[]{:S(2)}, u32[]{:S(2)}) collective-permute-start(bf16[16,8192]{1,0:T(8,128)(2,1)S(1)} %get-tuple-element.11), channel_id=1, source_target_pairs={{1,0},{2,1},{3,2},{0,3},{5,4},{6,5},{7,6},{4,7},{9,8},{10,9},{11,1... | collective-permute-start | bytes 786440 | tf_op jit(solution)/shard_map/ppermute | solution.py:405
  63.4 73.0 %collective-permute-start.2 = (bf16[16,8192]{1,0:T(8,128)(2,1)S(1)}, bf16[16,8192]{1,0:T(8,128)(2,1)S(1)}, u32[]{:S(2)}, u32[]{:S(2)}) collective-permute-start(bf16[16,8192]{1,0:T(8,128)(2,1)S(1)} %get-tuple-element.11), channel_id=1, source_target_pairs={{3,0},{0,1},{1,2},{2,3},{7,4},{4,5},{5,6},{6,7},{11,8},{8,9},{9,10... | collective-permute-start | bytes 786440 | tf_op jit(solution)/shard_map/ppermute | solution.py:405
  67.0 1.1 copy-start.1
  68.1 1.1 copy-start.2
  69.1 3.4 %copy-start.3 = (bf16[2,2,4,4,4,64,2,128]{7,6,5,4,3,2,1,0:T(2,128)(2,1)S(1)}, bf16[2,2,4,4,4,64,2,128]{7,6,5,4,3,2,1,0:T(2,128)(2,1)}, u32[]{:S(2)}) copy-start(bf16[2,2,4,4,4,64,2,128]{7,6,5,4,3,2,1,0:T(2,128)(2,1)} %get-tuple-element.6) | copy-start | bytes 25165828
  104.9 0.8 copy-start.5
  136.6 14.5 %copy-start.4 = (bf16[4,32,16,128]{3,2,1,0:T(8,128)(2,1)S(1)}, bf16[4,32,16,128]{3,2,1,0:T(8,128)(2,1)}, u32[]{:S(2)}) copy-start(bf16[4,32,16,128]{3,2,1,0:T(8,128)(2,1)} %get-tuple-element.8) | copy-start | bytes 1572868
  200.3 0.8 copy-start
Sparse Core Ops, SparseCore 0:
  60.0 51.7 all-gather.1

commit v3 on v0

v3 whole, which is shorter than its diff:
```python
import jax
import jax.numpy as jnp
from jax import lax
from jax.experimental import pallas as pl
from jax.experimental.pallas import tpu as pltpu
from jax.sharding import PartitionSpec as P

KS = 256
MIB = 2**20
MESH = pl.DeviceIdType.MESH
ROWS, SUBS = 32, 4
TILE, TILES = 1024, 8
ROUNDS = ((0, 1), (1, 3), (3, 4))
F32, BF16, I32 = jnp.float32, jnp.bfloat16, jnp.int32
TABLE = (2, 2, 4, 4, 4, 64, 2, 128)


def nt(a, b):
    return lax.dot_general(a, b, (((1,), (1,)), ((), ())), preferred_element_type=F32)


def step_kernel(
    ids, v, c, rot, codes, means, cross,
    tab1, tab2, near, stage1, stage2, vbuf, vr, got, turned, acc, part, partgot,
    chunk, bchunk, rounded, every, books, every_codes, resid, vcol, total, piece, piecegot,
    vsem, xs, xr, l1, s1, r1, l2, s2, r2, cs, cr, ps, pr, ms, mr, bs, br, ys, yr, ws, wr, vcsem,
):
    row = lax.axis_index("rows")
    sub = lax.axis_index("sub")
    core = lax.rem(row, 2)
    z = lax.rem(row // 2, 4)
    y = row // 8
    block = row // 8
    own = (sub == block).astype(I32)

    def up(i):
        return lax.rem(i + 1, 4)

    def down(i):
        return lax.rem(i + 3, 4)

    def device(at_y, at_z):
        return ((at_y * 4 + at_z) * 2 + core, sub)

    beside = (row + 1 - 2 * core, sub)
    after = ((device(up(y), z), device(down(y), z)), (device(y, up(z)), device(y, down(z))))
    across = ((row, up(sub)), (row, down(sub)))

    barrier = pltpu.get_barrier_semaphore()

    def greet(p, carry):
        to = lax.rem(row + p, ROWS)

        @pl.when(p > 0)
        def _():
            pl.semaphore_signal(barrier, inc=1, device_id=(to, sub), device_id_type=MESH)

        @pl.when(jnp.logical_or(p > 0, sub != block))
        def _():
            pl.semaphore_signal(barrier, inc=1, device_id=(to, block), device_id_type=MESH)

        return carry

    lax.fori_loop(0, ROWS, greet, 0)
    for p in range(1, SUBS):
        to = (row, lax.rem(sub + p, SUBS))
        pl.semaphore_signal(barrier, inc=1, device_id=to, device_id_type=MESH)

    def remote(src, dst, send, recv, to):
        return pltpu.make_async_remote_copy(
            src_ref=src, dst_ref=dst, send_sem=send, recv_sem=recv,
            device_id=to, device_id_type=MESH,
        )

    def v_copy(i):
        return pltpu.make_async_copy(
            v.at[pl.ds(i * TILE, TILE)], vbuf.at[lax.rem(i, 2)], vsem.at[lax.rem(i, 2)]
        )

    def turn_rows(first, last):
        def body(i, carry):
            v_copy(i).wait()

            @pl.when(i + 1 < TILES)
            def _():
                v_copy(i + 1).start()

            for h in range(2):
                value = jnp.dot(
                    vbuf[lax.rem(i, 2), h * 512:(h + 1) * 512, :], rot[...],
                    preferred_element_type=F32,
                )
                vr[pl.ds(pl.multiple_of(i * TILE + h * 512, 512), 512), :] = value
            return carry

        lax.fori_loop(first, last, body, 0)

    v_copy(0).start()
    turn_rows(0, 2)
    pl.semaphore_wait(barrier, 2 * ROWS + SUBS - 2 - own)

    def exchange(k):
        if k < 2:
            return remote(c, near.at[1 - k], xs.at[k], xr.at[k], across[k])
        half = pl.ds((k - 2) * 64, 64)
        return remote(near.at[3 - k, half], near.at[2, half], xs.at[k], xr.at[k], across[k - 2])

    class Gather:
        def __init__(self, table, stage, rounds, lsem, ssem, rsem):
            self.table, self.stage, self.rounds = table, stage, rounds
            self.lsem, self.ssem, self.rsem = lsem, ssem, rsem

        def hop(self, rnd, h, phase, k):
            first, last = self.rounds[rnd]
            qs = pl.ds(first, last - first)
            u, w = (y, z) if h == 0 else (z, y)
            to = after[h if phase == 0 else 1 - h][k % 2]
            at = ((rnd * 2 + h) * 2 + phase) * 4 + k
            mine = self.table.at[core, h]
            half = pl.ds(0, 32) if k == 2 else pl.ds(32, 32)
            if phase == 0:
                dst = mine.at[w, u, qs]
                if k < 2:
                    src = self.stage.at[qs, h]
                else:
                    src = dst = mine.at[w, down(u) if k == 2 else up(u), qs, half]
            elif k < 2:
                src = dst = mine.at[w, :, qs]
            else:
                src = dst = mine.at[down(w) if k == 2 else up(w), :, qs, half]
            return remote(src, dst, self.ssem.at[at], self.rsem.at[at], to)

        def keep(self, rnd, h):
            first, last = self.rounds[rnd]
            qs = pl.ds(first, last - first)
            u, w = (y, z) if h == 0 else (z, y)
            return pltpu.make_async_copy(
                self.stage.at[qs, h], self.table.at[core, h, w, u, qs], self.lsem.at[rnd * 2 + h]
            )

        def over(self, rnd, h):
            first, last = self.rounds[rnd]
            half = self.table.at[core, h, :, :, pl.ds(first, last - first)]
            at = len(self.rounds) * 16 + rnd * 2 + h
            return remote(half, half, self.ssem.at[at], self.rsem.at[at], beside)

        def start(self, rnd, phase):
            for k in range(2):
                for h in range(2):
                    self.hop(rnd, h, phase, k).start()

        def forward(self, rnd, phase):
            for k in range(2):
                for h in range(2):
                    self.hop(rnd, h, phase, k).wait_recv()
                    self.hop(rnd, h, phase, k + 2).start()

        def arrived(self, rnd, phase):
            for h in range(2):
                for k in (2, 3):
                    self.hop(rnd, h, phase, k).wait_recv()

        def begin(self, rnd):
            for h in range(2):
                self.keep(rnd, h).start()
            self.start(rnd, 0)

        def second(self, rnd):
            self.arrived(rnd, 0)
            for h in range(2):
                self.keep(rnd, h).wait()
            self.start(rnd, 1)

        def finish(self, rnd):
            self.arrived(rnd, 1)
            for h in range(2):
                self.over(rnd, h).start()

        def have(self):
            for rnd in range(len(self.rounds)):
                for h in range(2):
                    self.over(rnd, h).wait_recv()

        def drain(self):
            for rnd in range(len(self.rounds)):
                for h in range(2):
                    self.over(rnd, h).wait_send()
                    for phase in range(2):
                        for k in range(4):
                            self.hop(rnd, h, phase, k).wait_send()

    first_table = Gather(tab1, stage1, ROUNDS, l1, s1, r1)
    second_table = Gather(tab2, stage2, ((0, 4),), l2, s2, r2)
    first_column = pl.multiple_of(sub * 256, 256)

    def project(q, at):
        value = jnp.dot(at[...], rot[...], preferred_element_type=F32)
        stage1[q] = value.astype(BF16).reshape(2, 64, 2, 128)

    def columns(q, at):
        stage2[q] = at[:, pl.ds(first_column, 256)].reshape(2, 64, 2, 128)

    def share_codes(p):
        return remote(
            codes, every_codes.at[sub], cs.at[p], cr.at[sub], (row, lax.rem(sub + p, SUBS))
        )

    def shared_codes(p):
        source = lax.rem(sub + p, SUBS)
        return remote(codes, every_codes.at[source], cs.at[p], cr.at[source], (row, source))

    exchange(0).start()
    exchange(1).start()
    project(0, c)
    first_table.begin(0)
    own_codes = pltpu.make_async_copy(codes, every_codes.at[sub], cr.at[sub])
    own_codes.start()
    columns(0, c)
    turn_rows(2, 4)
    for k in range(2):
        exchange(k).wait_recv()
        exchange(k + 2).start()
    first_table.forward(0, 0)
    project(1, near.at[0])
    project(2, near.at[1])
    first_table.begin(1)
    first_table.second(0)
    exchange(2).wait_recv()
    exchange(3).wait_recv()
    project(3, near.at[2])
    first_table.begin(2)
    first_table.forward(1, 0)
    first_table.second(1)
    first_table.forward(2, 0)
    first_table.second(2)
    for p in range(1, SUBS):
        share_codes(p).start()
    first_table.forward(0, 1)
    turn_rows(4, 6)
    for q in range(3):
        columns(q + 1, near.at[q])
    first_table.finish(0)
    first_table.forward(1, 1)
    turn_rows(6, 8)
    first_table.finish(1)
    first_table.forward(2, 1)
    second_table.begin(0)
    acc[...] = jnp.zeros_like(acc)
    first_table.finish(2)
    first_table.have()
    second_table.forward(0, 0)

    def gather_rows(table, base, count, at):
        flat = table.reshape(16384, 2, 128)
        for s in range(0, count, 32):
            rows = [flat[ids[base + s + j]] for j in range(32)]
            for j in range(32):
                got[at + s + j] = rows[j]

    def gather_tile(table, i):
        def body(s, carry):
            gather_rows(table, i * TILE + s * 32, 32, s * 32)
            return carry

        lax.fori_loop(0, TILE // 32, body, 0)

    high = lax.broadcasted_iota(I32, (64, TILE), 0)
    low = lax.broadcasted_iota(I32, (4, TILE), 0)
    gather_tile(tab1, 0)

    def sum_tile(i, carry):
        @pl.when(i == 1)
        def _():
            second_table.second(0)

        @pl.when(i == 5)
        def _():
            second_table.forward(0, 1)

        at = pl.multiple_of(i * TILE, TILE)
        fetched = got[...].reshape(TILE, 256).astype(F32)
        rotated = vr[pl.ds(at, TILE), :] - fetched
        for h in range(2):
            turned[h * 128:(h + 1) * 128, :] = rotated[:, h * 128:(h + 1) * 128].T.astype(BF16)
        ahead = jnp.minimum(i + 1, TILES - 1) * TILE
        for grp in range(4):
            a, b, n = [], [], []
            for m in range(4 * grp, 4 * grp + 4):
                code = codes[m // 8, m % 8:m % 8 + 1, pl.ds(at, TILE)]
                a.append((high == (code & 63)).astype(BF16))
                mine = (low == (code >> 6)).astype(BF16)
                for l in range(4):
                    b.append(turned[m * 16:(m + 1) * 16, :] * mine[l:l + 1, :])
                n.append(mine)
            acc[grp] += nt(jnp.concatenate(b + n, axis=0), jnp.concatenate(a, axis=0))
            gather_rows(tab1, ahead + grp * 256, 256, grp * 256)
        return carry

    lax.fori_loop(0, TILES, sum_tile, 0)
    lane = lax.broadcasted_iota(I32, (1, 128), 1)
    for grp in range(4):
        for pair in range(2):
            cols = slice(pair * 128, pair * 128 + 128)
            m = 2 * pair
            both = jnp.where(
                lane < 64, acc[grp, m * 64:(m + 1) * 64, cols],
                acc[grp, (m + 1) * 64:(m + 2) * 64, cols],
            )
            count = jnp.where(
                lane < 64, acc[grp, 256 + m * 4:256 + m * 4 + 4, cols],
                acc[grp, 256 + m * 4 + 4:256 + m * 4 + 8, cols],
            )
            for l in range(4):
                at = (2 * grp + pair) * 4 + l
                part[at, :16, :] = both[l * 16:(l + 1) * 16, :]
                part[at, 16:, :] = jnp.broadcast_to(count[l:l + 1, :], (8, 128))

    def each(f, first=1):
        def body(p, carry):
            f(p)
            return carry

        lax.fori_loop(first, ROWS, body, 0)

    def scatter(p):
        to = lax.rem(row + p, ROWS)
        return remote(part.at[to], partgot.at[row], ps.at[p], pr.at[row], (to, sub))

    def scattered(p):
        source = lax.rem(row + p, ROWS)
        return remote(part.at[source], partgot.at[source], ps.at[p], pr.at[source], (source, sub))

    def give(p):
        to = lax.rem(row + p, ROWS)
        return remote(bchunk, rounded.at[row], bs.at[p], br.at[row], (to, sub))

    def given(p):
        source = lax.rem(row + p, ROWS)
        return remote(bchunk, rounded.at[source], bs.at[p], br.at[source], (source, sub))

    def publish(p):
        to = lax.rem(row + p, ROWS)
        return remote(chunk, means.at[row], ms.at[p], mr.at[row], (to, sub))

    def published(p):
        source = lax.rem(row + p, ROWS)
        return remote(chunk, means.at[source], ms.at[p], mr.at[source], (source, sub))

    def spread_books(p):
        to = (row, lax.rem(sub + p, SUBS))
        return remote(rounded, every.at[sub], ys.at[p], yr.at[sub], to)

    def spread_got(p):
        source = lax.rem(sub + p, SUBS)
        return remote(rounded, every.at[source], ys.at[p], yr.at[source], (row, source))

    def column_copy(i):
        return pltpu.make_async_copy(
            v.at[pl.ds(i * TILE, TILE), pl.ds(first_column, 256)],
            vcol.at[lax.rem(i, 2)], vcsem.at[lax.rem(i, 2)],
        )

    def residuals(first, last):
        def body(i, carry):
            gather_tile(tab2, i)
            column_copy(i).wait()

            @pl.when(i + 1 < TILES)
            def _():
                column_copy(i + 1).start()

            fetched = got[...].reshape(TILE, 256).astype(F32)
            value = (vcol[lax.rem(i, 2)].astype(F32) - fetched).T
            resid[:, pl.ds(pl.multiple_of(i * TILE, TILE), TILE)] = value.astype(BF16)
            return carry

        lax.fori_loop(first, last, body, 0)

    each(lambda p: scatter(p).start())
    column_copy(0).start()
    second_table.finish(0)

    def add(p, value):
        scattered(p).wait_recv()
        return value + partgot[lax.rem(row + p, ROWS)]

    value = lax.fori_loop(1, ROWS, add, part[row])
    mean = value[:16, :] / value[16:17, :]
    chunk[...] = mean
    bchunk[...] = mean.astype(BF16)
    means[row] = mean
    rounded[row] = mean.astype(BF16)
    each(lambda p: give(p).start())
    second_table.have()
    residuals(0, 4)
    each(lambda p: given(p).wait_recv())
    every[sub] = rounded[...]
    for p in range(1, SUBS):
        spread_books(p).start()
    each(lambda p: publish(p).start())
    residuals(4, 8)
    own_codes.wait()

    def send_piece(p, r):
        s = lax.rem(sub + p, SUBS)
        return remote(
            piece.at[r, p], piecegot.at[row], ws.at[p * 8 + r], wr.at[row], (sub * 8 + r, s)
        )

    def to_me(p, r):
        return jnp.logical_and(sub * 8 + r == row, p == 0)

    for p in range(SUBS):
        s = lax.rem(sub + p, SUBS)
        if p:
            spread_got(p).wait_recv()
            shared_codes(p).wait_recv()

        def relay(q, carry):
            for half in range(2):
                left = every[s, q * 4 + 2 * half].astype(F32)
                right = every[s, q * 4 + 2 * half + 1].astype(F32)
                books[2 * q, half] = jnp.where(lane < 64, left, pltpu.roll(right, 64, 1))
                books[2 * q + 1, half] = jnp.where(lane < 64, pltpu.roll(left, 64, 1), right)
            return carry

        lax.fori_loop(0, 8, relay, 0)
        total[...] = jnp.zeros_like(total)

        def cross_tile(i, carry):
            for quarter in range(TILE // 256):
                built = []
                at = pl.multiple_of(i * TILE + quarter * 256, 256)
                for m in range(16):
                    pieces = []
                    for t in range(2):
                        cols = pl.ds(pl.multiple_of(at + t * 128, 128), 128)
                        code = jnp.broadcast_to(every_codes[s, m // 8, m % 8:m % 8 + 1, cols], (8, 128))
                        inner = code & 127
                        both = []
                        for d in range(2):
                            low_half = books[m, 0, d * 8:(d + 1) * 8, :]
                            high_half = books[m, 1, d * 8:(d + 1) * 8, :]
                            both.append(jnp.where(
                                code >= 128,
                                jnp.take_along_axis(high_half, inner, axis=1),
                                jnp.take_along_axis(low_half, inner, axis=1),
                            ))
                        pieces.append(jnp.concatenate(both, axis=0).astype(BF16))
                    built.append(jnp.concatenate(pieces, axis=1))
                total[...] += nt(resid[:, pl.ds(at, 256)], jnp.concatenate(built, axis=0))
            return carry

        lax.fori_loop(0, TILES, cross_tile, 0)
        for r in range(8):
            piece[r, p] = (total[r * 32:(r + 1) * 32, :] * (1.0 / KS)).astype(BF16)
        for r in range(8):
            if p:
                send_piece(p, r).start()
            else:
                @pl.when(to_me(p, r))
                def _():
                    pltpu.make_async_copy(piece.at[r, p], piecegot.at[row], wr.at[row]).start()

                @pl.when(jnp.logical_not(to_me(p, r)))
                def _():
                    send_piece(p, r).start()

    def collect(p, value):
        source = lax.rem(row + p, ROWS)
        pltpu.make_async_copy(piece.at[0, 0], piecegot.at[source], wr.at[source]).wait()
        return value + piecegot[source].astype(F32)

    cross[...] = lax.fori_loop(0, ROWS, collect, jnp.zeros(cross.shape, F32))

    for k in range(4):
        exchange(k).wait_send()
    first_table.drain()
    second_table.drain()
    for p in range(1, SUBS):
        share_codes(p).wait_send()
        spread_books(p).wait_send()
    each(lambda p: published(p).wait_recv())
    each(lambda p: scatter(p).wait_send())
    each(lambda p: give(p).wait_send())
    each(lambda p: publish(p).wait_send())
    for p in range(SUBS):
        for r in range(8):
            if p:
                send_piece(p, r).wait_send()
            else:
                @pl.when(jnp.logical_not(to_me(p, r)))
                def _():
                    send_piece(p, r).wait_send()


def step_call(ids, vectors, centroids, rotation, codes):
    vmem = pl.BlockSpec(memory_space=pltpu.VMEM)
    dma = pltpu.SemaphoreType.DMA
    return pl.pallas_call(
        step_kernel,
        out_shape=(
            jax.ShapeDtypeStruct((ROWS, 16, 128), F32),
            jax.ShapeDtypeStruct((32, 256), F32),
        ),
        in_specs=[
            pl.BlockSpec(memory_space=pltpu.SMEM),
            pl.BlockSpec(memory_space=pl.ANY),
            vmem, vmem, vmem,
        ],
        out_specs=(vmem, vmem),
        scratch_shapes=[
            pltpu.VMEM(TABLE, BF16),
            pltpu.VMEM(TABLE, BF16),
            pltpu.VMEM((3, 128, 1024), BF16),
            pltpu.VMEM((4, 2, 64, 2, 128), BF16),
            pltpu.VMEM((4, 2, 64, 2, 128), BF16),
            pltpu.VMEM((2, TILE, 1024), BF16),
            pltpu.VMEM((TILE * TILES, 256), F32),
            pltpu.VMEM((TILE, 2, 128), BF16),
            pltpu.VMEM((256, TILE), BF16),
            pltpu.VMEM((4, 272, 256), F32),
            pltpu.VMEM((ROWS, 24, 128), F32),
            pltpu.VMEM((ROWS, 24, 128), F32),
            pltpu.VMEM((16, 128), F32),
            pltpu.VMEM((16, 128), BF16),
            pltpu.VMEM((ROWS, 16, 128), BF16),
            pltpu.VMEM((SUBS, ROWS, 16, 128), BF16),
            pltpu.VMEM((16, 2, 16, 128), F32),
            pltpu.VMEM((SUBS, 2, 8, TILE * TILES), I32),
            pltpu.VMEM((256, TILE * TILES), BF16),
            pltpu.VMEM((2, TILE, 256), BF16),
            pltpu.VMEM((256, 256), F32),
            pltpu.VMEM((8, SUBS, 32, 256), BF16),
            pltpu.VMEM((ROWS, 32, 256), BF16),
            dma((2,)), dma((4,)), dma((4,)),
            dma((6,)), dma((54,)), dma((54,)),
            dma((2,)), dma((18,)), dma((18,)),
            dma((SUBS,)), dma((SUBS,)),
            dma((ROWS,)), dma((ROWS,)),
            dma((ROWS,)), dma((ROWS,)),
            dma((ROWS,)), dma((ROWS,)),
            dma((SUBS,)), dma((SUBS,)),
            dma((ROWS,)), dma((ROWS,)),
            dma((2,)),
        ],
        compiler_params=pltpu.CompilerParams(
            collective_id=1, has_side_effects=True, vmem_limit_bytes=56 * MIB
        ),
        cost_estimate=pl.CostEstimate(
            flops=20 * 10**9, bytes_accessed=40 * 10**6, transcendentals=0
        ),
        name="step",
    )(ids, vectors, centroids, rotation, codes)


def local(vectors, list_ids, centroids, rotation, codes):
    sub = lax.axis_index("sub")
    owner, inner = list_ids // 128, list_ids % 128
    at_row, at_sub = owner // 4, owner % 4
    apart = (at_sub - sub + 4) % 4
    near = jnp.where(apart < 2, apart, 5 - apart)
    at_y, at_z, at_core = at_row // 8, (at_row // 2) % 4, at_row % 2
    half = inner // 64
    block = jnp.where(half == 0, at_z * 4 + at_y, at_y * 4 + at_z)
    ids = (((at_core * 2 + half) * 16 + block) * 4 + near) * 64 + inner % 64
    means, cross_cov = step_call(
        ids, vectors, centroids, rotation, codes.reshape(2, 8, -1)
    )
    codebooks = means.reshape(8, 4, 16, 2, 64).transpose(0, 3, 1, 4, 2).reshape(16, 256, 16)
    return codebooks, cross_cov


def solution(mesh):
    placed = (
        P("rows", None),
        P("rows"),
        P(("rows", "sub"), None),
        P(None, "sub"),
        P("sub", "rows"),
    )
    return jax.shard_map(
        local,
        mesh=mesh,
        in_specs=placed,
        out_specs=(P("sub", None, None), P("rows", "sub")),
        check_vma=False,
    )
```

time: 662 us -> 151 us (0.23); the launches traced: 655 us -> 151 us
  waiting for transfers between devices: 189 us -> 0 us
  local copies, waits for them, and re-layouts: 182 us -> 4.03 us
  Pallas kernels: 0 us -> 145 us
  blocking collectives: 121 us -> 0 us
  matrix products: 112 us -> 0 us
  other arithmetic: 25.8 us -> 1.55 us
  between operations: 13.8 us -> 0.66 us
  loops' own time: 10.1 us -> 0 us
    gather x1 -> x0, local copies, waits for them, and re-layouts: 150 us -> none  [local(): fetched = jnp.take(centre_table, list_ids, axis=0)]
    pallas_call x0 -> x1, Pallas kernels: none -> 145 us  [step_call(): pl.pallas_call(step_kernel, out_shape=(jax.ShapeDtypeStruct((ROWS, 16, 12...]
    psum x1 -> x0, blocking collectives: 121 us -> none  [local(): code_sums, counts = lax.psum((code_sums, counts), 'rows')]
    dot_general x18 -> x0, matrix products: 112 us -> none  [the longest x8 46.9 us: accumulate(): jnp.einsum('mrk,rmd->mkd', onehot, piece_block, preferred_element_type=jn...]
    all_gather x1 -> x0, waiting for transfers between devices: 111 us -> none  [local(): lax.all_gather(centroids, ('rows', 'sub'), axis=0, tiled=True)]
    reduce_scatter x1 -> x0, waiting for transfers between devices: 77.4 us -> none  [local(): lax.psum_scatter(jnp.dot(residual.T, rebuilt, preferred_element_type=jnp....]
    dynamic_slice x32 -> x0, local copies, waits for them, and re-layouts: 22.9 us -> none  [the longest x16 9.29 us: local(): lax.scan(accumulate, (start_sums, start_counts), jnp.arange(block_count,...]
    reduce_sum x8 -> x0, other arithmetic: 22.5 us -> none  [accumulate(): counts = counts + jnp.sum(onehot, axis=1, dtype=jnp.float32)]
  transfers between devices with their start and end apart: 3 -> 0, of which waited for: 2 -> 0; matrix products, arithmetic and copies ran while one was open for 0% -> 0% of each run, Pallas kernels for 0% -> 0%
where the time goes in v3:
time: 151 us
  Pallas kernels  145 us (96%)
  local copies, waits for them, and re-layouts  4.03 us (3%)
  other arithmetic  1.55 us (1%)
    pallas_call x1, Pallas kernels, step_call(): pl.pallas_call(step_kernel, out_shape=(jax.ShapeDtypeStruct((ROWS, 16, 12...  145 us

profile of v3, /device:TPU:7, one launch (start us, length us, event | category | flops | bytes accessed | tf_op | source)
XLA Modules:
  0.0 151.0 jit_solution(15564548430448057258)
XLA Ops:
  0.6 1.6 %fusion.7.ids = s32[8192]{0:T(1024)} fusion(s32[8192]{0:T(1024)} %param.6, s32[]{:T(128)S(6)} %axis_index.12), kind=kLoop, calls=%fused_computation.37 | loop fusion | flops 1040384 | bytes 65540 | tf_op jit(solution)/shard_map/add | solution.py:566
  2.2 144.8 %step.1 = (f32[32,16,128]{2,1,0:T(8,128)}, f32[32,256]{1,0:T(8,128)}) custom-call(s32[8192]{0:T(1024)} %fusion.7.ids, bf16[8192,1024]{1,0:T(8,128)(2,1)} %v.1, bf16[128,1024]{1,0:T(8,128)(2,1)} %c.1, bf16[1024,256]{1,0:T(8,128)(2,1)} %rot.1, s32[2,8,8192]{2,1,0:T(8,128)} %bitcast.5), custom_call_target="tpu_custom_call" | custom-call | flops 20000000000 | bytes 40000000 | tf_op jit(solution)/shard_map/step/pallas_call | solution.py:500
  147.0 1.3 reshape.14
  148.2 0.3 copy.7
  148.6 1.0 reshape.15
  149.6 1.4 copy.9

commit v4 on v3

--- a/solution.py
+++ b/solution.py
@@ -96,14 +96,17 @@
         lax.fori_loop(first, last, body, 0)
 
     v_copy(0).start()
-    turn_rows(0, 2)
+    turn_rows(0, 3)
     pl.semaphore_wait(barrier, 2 * ROWS + SUBS - 2 - own)
 
     def exchange(k):
-        if k < 2:
-            return remote(c, near.at[1 - k], xs.at[k], xr.at[k], across[k])
-        half = pl.ds((k - 2) * 64, 64)
-        return remote(near.at[3 - k, half], near.at[2, half], xs.at[k], xr.at[k], across[k - 2])
+        half = pl.ds((0, 64, 64, 0, 0, 64)[k], 64)
+        from_up = k % 2
+        if k < 4:
+            src, dst = c.at[half], near.at[1 - from_up, half]
+        else:
+            src, dst = near.at[1 - from_up, half], near.at[2, half]
+        return remote(src, dst, xs.at[k], xr.at[k], across[from_up])
 
     class Gather:
         def __init__(self, table, stage, rounds, lsem, ssem, rsem):
@@ -138,11 +141,13 @@
                 self.stage.at[qs, h], self.table.at[core, h, w, u, qs], self.lsem.at[rnd * 2 + h]
             )
 
-        def over(self, rnd, h):
+        def over(self, rnd, h, j):
             first, last = self.rounds[rnd]
-            half = self.table.at[core, h, :, :, pl.ds(first, last - first)]
-            at = len(self.rounds) * 16 + rnd * 2 + h
-            return remote(half, half, self.ssem.at[at], self.rsem.at[at], beside)
+            w = z if h == 0 else y
+            w = (w, down(w), up(w), lax.rem(w + 2, 4))[j]
+            blocks = self.table.at[core, h, w, :, pl.ds(first, last - first)]
+            at = len(self.rounds) * 16 + (rnd * 2 + h) * 4 + j
+            return remote(blocks, blocks, self.ssem.at[at], self.rsem.at[at], beside)
 
         def start(self, rnd, phase):
             for k in range(2):
@@ -154,6 +159,8 @@
                 for h in range(2):
                     self.hop(rnd, h, phase, k).wait_recv()
                     self.hop(rnd, h, phase, k + 2).start()
+                    if phase == 1:
+                        self.over(rnd, h, k + 1).start()
 
         def arrived(self, rnd, phase):
             for h in range(2):
@@ -170,27 +177,31 @@
             for h in range(2):
                 self.keep(rnd, h).wait()
             self.start(rnd, 1)
+            for h in range(2):
+                self.over(rnd, h, 0).start()
 
         def finish(self, rnd):
             self.arrived(rnd, 1)
             for h in range(2):
-                self.over(rnd, h).start()
+                self.over(rnd, h, 3).start()
 
         def have(self):
             for rnd in range(len(self.rounds)):
                 for h in range(2):
-                    self.over(rnd, h).wait_recv()
+                    for j in range(4):
+                        self.over(rnd, h, j).wait_recv()
 
         def drain(self):
             for rnd in range(len(self.rounds)):
                 for h in range(2):
-                    self.over(rnd, h).wait_send()
+                    for j in range(4):
+                        self.over(rnd, h, j).wait_send()
                     for phase in range(2):
                         for k in range(4):
                             self.hop(rnd, h, phase, k).wait_send()
 
     first_table = Gather(tab1, stage1, ROUNDS, l1, s1, r1)
-    second_table = Gather(tab2, stage2, ((0, 4),), l2, s2, r2)
+    second_table = Gather(tab2, stage2, ((0, 1), (1, 4)), l2, s2, r2)
     first_column = pl.multiple_of(sub * 256, 256)
 
     def project(q, at):
@@ -209,24 +220,30 @@
         source = lax.rem(sub + p, SUBS)
         return remote(codes, every_codes.at[source], cs.at[p], cr.at[source], (row, source))
 
-    exchange(0).start()
-    exchange(1).start()
+    for k in range(4):
+        exchange(k).start()
     project(0, c)
     first_table.begin(0)
+    columns(0, c)
+    second_table.begin(0)
     own_codes = pltpu.make_async_copy(codes, every_codes.at[sub], cr.at[sub])
     own_codes.start()
-    columns(0, c)
-    turn_rows(2, 4)
+    first_table.forward(0, 0)
+    second_table.forward(0, 0)
+    first_table.second(0)
+    second_table.second(0)
     for k in range(2):
         exchange(k).wait_recv()
-        exchange(k + 2).start()
-    first_table.forward(0, 0)
+        exchange(k + 4).start()
+    turn_rows(3, 4)
+    exchange(2).wait_recv()
+    exchange(3).wait_recv()
     project(1, near.at[0])
     project(2, near.at[1])
     first_table.begin(1)
-    first_table.second(0)
-    exchange(2).wait_recv()
-    exchange(3).wait_recv()
+    first_table.forward(0, 1)
+    exchange(4).wait_recv()
+    exchange(5).wait_recv()
     project(3, near.at[2])
     first_table.begin(2)
     first_table.forward(1, 0)
@@ -235,20 +252,21 @@
     first_table.second(2)
     for p in range(1, SUBS):
         share_codes(p).start()
-    first_table.forward(0, 1)
-    turn_rows(4, 6)
+    first_table.finish(0)
+    second_table.forward(0, 1)
     for q in range(3):
         columns(q + 1, near.at[q])
-    first_table.finish(0)
+    turn_rows(4, 6)
+    second_table.finish(0)
     first_table.forward(1, 1)
     turn_rows(6, 8)
     first_table.finish(1)
     first_table.forward(2, 1)
-    second_table.begin(0)
+    second_table.begin(1)
     acc[...] = jnp.zeros_like(acc)
     first_table.finish(2)
     first_table.have()
-    second_table.forward(0, 0)
+    second_table.forward(1, 0)
 
     def gather_rows(table, base, count, at):
         flat = table.reshape(16384, 2, 128)
@@ -271,11 +289,11 @@
     def sum_tile(i, carry):
         @pl.when(i == 1)
         def _():
-            second_table.second(0)
-
-        @pl.when(i == 5)
+            second_table.second(1)
+
+        @pl.when(i == 6)
         def _():
-            second_table.forward(0, 1)
+            second_table.forward(1, 1)
 
         at = pl.multiple_of(i * TILE, TILE)
         fetched = got[...].reshape(TILE, 256).astype(F32)
@@ -313,7 +331,7 @@
             for l in range(4):
                 at = (2 * grp + pair) * 4 + l
                 part[at, :16, :] = both[l * 16:(l + 1) * 16, :]
-                part[at, 16:, :] = jnp.broadcast_to(count[l:l + 1, :], (8, 128))
+                part[at, 16:17, :] = count[l:l + 1, :]
 
     def each(f, first=1):
         def body(p, carry):
@@ -324,11 +342,16 @@
 
     def scatter(p):
         to = lax.rem(row + p, ROWS)
-        return remote(part.at[to], partgot.at[row], ps.at[p], pr.at[row], (to, sub))
+        return remote(
+            part.at[to, pl.ds(0, 17)], partgot.at[row, pl.ds(0, 17)], ps.at[p], pr.at[row], (to, sub)
+        )
 
     def scattered(p):
         source = lax.rem(row + p, ROWS)
-        return remote(part.at[source], partgot.at[source], ps.at[p], pr.at[source], (source, sub))
+        return remote(
+            part.at[source, pl.ds(0, 17)], partgot.at[source, pl.ds(0, 17)], ps.at[p], pr.at[source],
+            (source, sub),
+        )
 
     def give(p):
         to = lax.rem(row + p, ROWS)
@@ -360,31 +383,15 @@
             vcol.at[lax.rem(i, 2)], vcsem.at[lax.rem(i, 2)],
         )
 
-    def residuals(first, last):
-        def body(i, carry):
-            gather_tile(tab2, i)
-            column_copy(i).wait()
-
-            @pl.when(i + 1 < TILES)
-            def _():
-                column_copy(i + 1).start()
-
-            fetched = got[...].reshape(TILE, 256).astype(F32)
-            value = (vcol[lax.rem(i, 2)].astype(F32) - fetched).T
-            resid[:, pl.ds(pl.multiple_of(i * TILE, TILE), TILE)] = value.astype(BF16)
-            return carry
-
-        lax.fori_loop(first, last, body, 0)
-
     each(lambda p: scatter(p).start())
     column_copy(0).start()
-    second_table.finish(0)
+    second_table.finish(1)
 
     def add(p, value):
         scattered(p).wait_recv()
-        return value + partgot[lax.rem(row + p, ROWS)]
-
-    value = lax.fori_loop(1, ROWS, add, part[row])
+        return value + partgot[lax.rem(row + p, ROWS), :17, :]
+
+    value = lax.fori_loop(1, ROWS, add, part[row, :17, :])
     mean = value[:16, :] / value[16:17, :]
     chunk[...] = mean
     bchunk[...] = mean.astype(BF16)
@@ -392,13 +399,12 @@
     rounded[row] = mean.astype(BF16)
     each(lambda p: give(p).start())
     second_table.have()
-    residuals(0, 4)
+    gather_tile(tab2, 0)
     each(lambda p: given(p).wait_recv())
     every[sub] = rounded[...]
     for p in range(1, SUBS):
         spread_books(p).start()
     each(lambda p: publish(p).start())
-    residuals(4, 8)
     own_codes.wait()
 
     def send_piece(p, r):
@@ -428,6 +434,18 @@
         total[...] = jnp.zeros_like(total)
 
         def cross_tile(i, carry):
+            if p == 0:
+                column_copy(i).wait()
+
+                @pl.when(i + 1 < TILES)
+                def _():
+                    column_copy(i + 1).start()
+
+                fetched = got[...].reshape(TILE, 256).astype(F32)
+                value = (vcol[lax.rem(i, 2)].astype(F32) - fetched).T
+                resid[:, pl.ds(pl.multiple_of(i * TILE, TILE), TILE)] = value.astype(BF16)
+                ahead = jnp.minimum(i + 1, TILES - 1) * TILE
+
             for quarter in range(TILE // 256):
                 built = []
                 at = pl.multiple_of(i * TILE + quarter * 256, 256)
@@ -449,6 +467,8 @@
                         pieces.append(jnp.concatenate(both, axis=0).astype(BF16))
                     built.append(jnp.concatenate(pieces, axis=1))
                 total[...] += nt(resid[:, pl.ds(at, 256)], jnp.concatenate(built, axis=0))
+                if p == 0:
+                    gather_rows(tab2, ahead + quarter * 256, 256, quarter * 256)
             return carry
 
         lax.fori_loop(0, TILES, cross_tile, 0)
@@ -473,7 +493,7 @@
 
     cross[...] = lax.fori_loop(0, ROWS, collect, jnp.zeros(cross.shape, F32))
 
-    for k in range(4):
+    for k in range(6):
         exchange(k).wait_send()
     first_table.drain()
     second_table.drain()
@@ -533,9 +553,9 @@
             pltpu.VMEM((256, 256), F32),
             pltpu.VMEM((8, SUBS, 32, 256), BF16),
             pltpu.VMEM((ROWS, 32, 256), BF16),
-            dma((2,)), dma((4,)), dma((4,)),
-            dma((6,)), dma((54,)), dma((54,)),
-            dma((2,)), dma((18,)), dma((18,)),
+            dma((2,)), dma((6,)), dma((6,)),
+            dma((6,)), dma((72,)), dma((72,)),
+            dma((4,)), dma((48,)), dma((48,)),
             dma((SUBS,)), dma((SUBS,)),
             dma((ROWS,)), dma((ROWS,)),
             dma((ROWS,)), dma((ROWS,)),

time: 151 us -> 147 us (0.974)
  Pallas kernels: 145 us -> 141 us
    pallas_call x1, Pallas kernels: 145 us -> 141 us  [step_call(): pl.pallas_call(step_kernel, out_shape=(jax.ShapeDtypeStruct((ROWS, 16, 12...]
where the time goes in v4:
time: 147 us
  Pallas kernels  141 us (96%)
  local copies, waits for them, and re-layouts  4.03 us (3%)
  other arithmetic  1.55 us (1%)
    pallas_call x1, Pallas kernels, step_call(): pl.pallas_call(step_kernel, out_shape=(jax.ShapeDtypeStruct((ROWS, 16, 12...  141 us

profile of v4, /device:TPU:7, one launch (start us, length us, event | category | flops | bytes accessed | tf_op | source)
XLA Modules:
  0.0 146.8 jit_solution(17077957856140940388)
XLA Ops:
  0.6 1.6 %fusion.7.ids = s32[8192]{0:T(1024)} fusion(s32[8192]{0:T(1024)} %param.6, s32[]{:T(128)S(6)} %axis_index.12), kind=kLoop, calls=%fused_computation.37 | loop fusion | flops 1040384 | bytes 65540 | tf_op jit(solution)/shard_map/add | solution.py:586
  2.2 140.6 %step.1 = (f32[32,16,128]{2,1,0:T(8,128)}, f32[32,256]{1,0:T(8,128)}) custom-call(s32[8192]{0:T(1024)} %fusion.7.ids, bf16[8192,1024]{1,0:T(8,128)(2,1)} %v.1, bf16[128,1024]{1,0:T(8,128)(2,1)} %c.1, bf16[1024,256]{1,0:T(8,128)(2,1)} %rot.1, s32[2,8,8192]{2,1,0:T(8,128)} %bitcast.5), custom_call_target="tpu_custom_call" | custom-call | flops 20000000000 | bytes 40000000 | tf_op jit(solution)/shard_map/step/pallas_call | solution.py:520
  142.8 1.3 reshape.14
  144.0 0.3 copy.7
  144.4 1.0 reshape.15
  145.4 1.4 copy.9

commit v5 on v4

--- a/solution.py
+++ b/solution.py
@@ -20,10 +20,11 @@
 
 
 def step_kernel(
-    ids, v, c, rot, codes, means, cross,
-    tab1, tab2, near, stage1, stage2, vbuf, vr, got, turned, acc, part, partgot,
+    ids, v, c, rot, codes, outbooks, cross,
+    tab1, tab2, near, stage1, stage2, vbuf, vr, got, turned, acc, part, partgot, means,
     chunk, bchunk, rounded, every, books, every_codes, resid, vcol, total, piece, piecegot,
-    vsem, xs, xr, l1, s1, r1, l2, s2, r2, cs, cr, ps, pr, ms, mr, bs, br, ys, yr, ws, wr, vcsem,
+    vsem, xs, xr, l1, s1, r1, o1, l2, s2, r2, o2, cs, cr, ps, pr, ms, mr, bs, br, ys, yr, ws, wr,
+    vcsem,
 ):
     row = lax.axis_index("rows")
     sub = lax.axis_index("sub")
@@ -31,7 +32,6 @@
     z = lax.rem(row // 2, 4)
     y = row // 8
     block = row // 8
-    own = (sub == block).astype(I32)
 
     def up(i):
         return lax.rem(i + 1, 4)
@@ -47,24 +47,8 @@
     across = ((row, up(sub)), (row, down(sub)))
 
     barrier = pltpu.get_barrier_semaphore()
-
-    def greet(p, carry):
-        to = lax.rem(row + p, ROWS)
-
-        @pl.when(p > 0)
-        def _():
-            pl.semaphore_signal(barrier, inc=1, device_id=(to, sub), device_id_type=MESH)
-
-        @pl.when(jnp.logical_or(p > 0, sub != block))
-        def _():
-            pl.semaphore_signal(barrier, inc=1, device_id=(to, block), device_id_type=MESH)
-
-        return carry
-
-    lax.fori_loop(0, ROWS, greet, 0)
-    for p in range(1, SUBS):
-        to = (row, lax.rem(sub + p, SUBS))
-        pl.semaphore_signal(barrier, inc=1, device_id=to, device_id_type=MESH)
+    for peer in after[0] + after[1] + across + (beside,):
+        pl.semaphore_signal(barrier, inc=1, device_id=peer, device_id_type=MESH)
 
     def remote(src, dst, send, recv, to):
         return pltpu.make_async_remote_copy(
@@ -97,7 +81,7 @@
 
     v_copy(0).start()
     turn_rows(0, 3)
-    pl.semaphore_wait(barrier, 2 * ROWS + SUBS - 2 - own)
+    pl.semaphore_wait(barrier, 7)
 
     def exchange(k):
         half = pl.ds((0, 64, 64, 0, 0, 64)[k], 64)
@@ -109,99 +93,109 @@
         return remote(src, dst, xs.at[k], xr.at[k], across[from_up])
 
     class Gather:
-        def __init__(self, table, stage, rounds, lsem, ssem, rsem):
+        def __init__(self, table, stage, rounds, lsem, ssem, rsem, osem):
             self.table, self.stage, self.rounds = table, stage, rounds
-            self.lsem, self.ssem, self.rsem = lsem, ssem, rsem
-
-        def hop(self, rnd, h, phase, k):
+            self.lsem, self.ssem, self.rsem, self.osem = lsem, ssem, rsem, osem
+
+        def place(self, rnd, h):
             first, last = self.rounds[rnd]
-            qs = pl.ds(first, last - first)
             u, w = (y, z) if h == 0 else (z, y)
+            return pl.ds(first, last - first), u, w
+
+        def hop(self, rnd, h, phase, k, j=0):
+            qs, u, w = self.place(rnd, h)
             to = after[h if phase == 0 else 1 - h][k % 2]
-            at = ((rnd * 2 + h) * 2 + phase) * 4 + k
             mine = self.table.at[core, h]
             half = pl.ds(0, 32) if k == 2 else pl.ds(32, 32)
             if phase == 0:
-                dst = mine.at[w, u, qs]
                 if k < 2:
-                    src = self.stage.at[qs, h]
+                    src, dst = self.stage.at[qs, h], mine.at[w, u, qs]
                 else:
                     src = dst = mine.at[w, down(u) if k == 2 else up(u), qs, half]
-            elif k < 2:
-                src = dst = mine.at[w, :, qs]
             else:
-                src = dst = mine.at[down(w) if k == 2 else up(w), :, qs, half]
-            return remote(src, dst, self.ssem.at[at], self.rsem.at[at], to)
+                at = (u, down(u), up(u), lax.rem(u + 2, 4))[j]
+                if k < 2:
+                    src, dst = mine.at[w, at, qs], mine.at[w, at, qs]
+                    if j == 0:
+                        src = self.stage.at[qs, h]
+                else:
+                    src = dst = mine.at[down(w) if k == 2 else up(w), at, qs, half]
+            number = (rnd * 2 + h) * 20 + (k if phase == 0 else 4 + 4 * j + k)
+            return remote(src, dst, self.ssem.at[phase], self.rsem.at[number], to)
 
         def keep(self, rnd, h):
-            first, last = self.rounds[rnd]
-            qs = pl.ds(first, last - first)
-            u, w = (y, z) if h == 0 else (z, y)
+            qs, u, w = self.place(rnd, h)
             return pltpu.make_async_copy(
                 self.stage.at[qs, h], self.table.at[core, h, w, u, qs], self.lsem.at[rnd * 2 + h]
             )
 
         def over(self, rnd, h, j):
-            first, last = self.rounds[rnd]
-            w = z if h == 0 else y
+            qs, u, w = self.place(rnd, h)
             w = (w, down(w), up(w), lax.rem(w + 2, 4))[j]
-            blocks = self.table.at[core, h, w, :, pl.ds(first, last - first)]
-            at = len(self.rounds) * 16 + (rnd * 2 + h) * 4 + j
-            return remote(blocks, blocks, self.ssem.at[at], self.rsem.at[at], beside)
-
-        def start(self, rnd, phase):
-            for k in range(2):
-                for h in range(2):
-                    self.hop(rnd, h, phase, k).start()
-
-        def forward(self, rnd, phase):
-            for k in range(2):
-                for h in range(2):
-                    self.hop(rnd, h, phase, k).wait_recv()
-                    self.hop(rnd, h, phase, k + 2).start()
-                    if phase == 1:
-                        self.over(rnd, h, k + 1).start()
-
-        def arrived(self, rnd, phase):
-            for h in range(2):
-                for k in (2, 3):
-                    self.hop(rnd, h, phase, k).wait_recv()
+            blocks = self.table.at[core, h, w, :, qs]
+            remote(blocks, blocks, self.osem.at[0], self.osem.at[1], beside).start()
 
         def begin(self, rnd):
             for h in range(2):
                 self.keep(rnd, h).start()
-            self.start(rnd, 0)
-
-        def second(self, rnd):
-            self.arrived(rnd, 0)
+            for h in range(2):
+                for k in range(2):
+                    self.hop(rnd, h, 0, k).start()
+            for h in range(2):
+                for k in range(2):
+                    self.hop(rnd, h, 1, k).start()
+
+        def sides(self, rnd):
+            for k in range(2):
+                for h in range(2):
+                    self.hop(rnd, h, 0, k).wait_recv()
+                    self.hop(rnd, h, 0, k + 2).start()
+            for j in (1, 2):
+                for h in range(2):
+                    for k in range(2):
+                        self.hop(rnd, h, 1, k, j).start()
+
+        def opposite(self, rnd):
+            for h in range(2):
+                for k in (2, 3):
+                    self.hop(rnd, h, 0, k).wait_recv()
+                for k in range(2):
+                    self.hop(rnd, h, 1, k, 3).start()
             for h in range(2):
                 self.keep(rnd, h).wait()
-            self.start(rnd, 1)
+                self.over(rnd, h, 0)
+
+        def forward(self, rnd, *blocks):
+            for j in blocks:
+                for k in range(2):
+                    for h in range(2):
+                        self.hop(rnd, h, 1, k, j).wait_recv()
+                        self.hop(rnd, h, 1, k + 2, j).start()
+            if blocks[-1] == 3:
+                for h in range(2):
+                    self.over(rnd, h, 1)
+                    self.over(rnd, h, 2)
+
+        def finish(self, rnd):
             for h in range(2):
-                self.over(rnd, h, 0).start()
-
-        def finish(self, rnd):
-            self.arrived(rnd, 1)
-            for h in range(2):
-                self.over(rnd, h, 3).start()
+                for j in range(4):
+                    for k in (2, 3):
+                        self.hop(rnd, h, 1, k, j).wait_recv()
+                self.over(rnd, h, 3)
+
+        def all_of(self, blocks, sem):
+            pltpu.make_async_copy(blocks, blocks, sem).wait()
 
         def have(self):
-            for rnd in range(len(self.rounds)):
-                for h in range(2):
-                    for j in range(4):
-                        self.over(rnd, h, j).wait_recv()
+            self.all_of(self.table.at[0], self.osem.at[1])
 
         def drain(self):
-            for rnd in range(len(self.rounds)):
-                for h in range(2):
-                    for j in range(4):
-                        self.over(rnd, h, j).wait_send()
-                    for phase in range(2):
-                        for k in range(4):
-                            self.hop(rnd, h, phase, k).wait_send()
-
-    first_table = Gather(tab1, stage1, ROUNDS, l1, s1, r1)
-    second_table = Gather(tab2, stage2, ((0, 1), (1, 4)), l2, s2, r2)
+            self.all_of(self.table.at[0, :, 0, pl.ds(0, 3)], self.ssem.at[0])
+            self.all_of(self.table.at[0, :, pl.ds(0, 3)], self.ssem.at[1])
+            self.all_of(self.table.at[0], self.osem.at[0])
+
+    first_table = Gather(tab1, stage1, ROUNDS, l1, s1, r1, o1)
+    second_table = Gather(tab2, stage2, ((0, 4),), l2, s2, r2, o2)
     first_column = pl.multiple_of(sub * 256, 256)
 
     def project(q, at):
@@ -213,60 +207,61 @@
 
     def share_codes(p):
         return remote(
-            codes, every_codes.at[sub], cs.at[p], cr.at[sub], (row, lax.rem(sub + p, SUBS))
+            codes, every_codes.at[sub], cs.at[0], cr.at[sub], (row, lax.rem(sub + p, SUBS))
         )
 
     def shared_codes(p):
         source = lax.rem(sub + p, SUBS)
-        return remote(codes, every_codes.at[source], cs.at[p], cr.at[source], (row, source))
+        return remote(codes, every_codes.at[source], cs.at[0], cr.at[source], (row, source))
 
     for k in range(4):
         exchange(k).start()
     project(0, c)
     first_table.begin(0)
-    columns(0, c)
-    second_table.begin(0)
     own_codes = pltpu.make_async_copy(codes, every_codes.at[sub], cr.at[sub])
     own_codes.start()
-    first_table.forward(0, 0)
-    second_table.forward(0, 0)
-    first_table.second(0)
-    second_table.second(0)
+    columns(0, c)
+    first_table.sides(0)
+    first_table.opposite(0)
     for k in range(2):
         exchange(k).wait_recv()
         exchange(k + 4).start()
     turn_rows(3, 4)
+    first_table.forward(0, 0)
     exchange(2).wait_recv()
     exchange(3).wait_recv()
     project(1, near.at[0])
     project(2, near.at[1])
     first_table.begin(1)
-    first_table.forward(0, 1)
+    first_table.forward(0, 1, 2)
     exchange(4).wait_recv()
     exchange(5).wait_recv()
     project(3, near.at[2])
     first_table.begin(2)
-    first_table.forward(1, 0)
-    first_table.second(1)
-    first_table.forward(2, 0)
-    first_table.second(2)
+    first_table.sides(1)
+    first_table.sides(2)
+    first_table.forward(0, 3)
+    turn_rows(4, 5)
+    first_table.opposite(1)
+    first_table.opposite(2)
     for p in range(1, SUBS):
         share_codes(p).start()
-    first_table.finish(0)
-    second_table.forward(0, 1)
+    turn_rows(5, 6)
+    first_table.forward(1, 0)
+    first_table.forward(2, 0)
+    first_table.forward(1, 1, 2)
+    first_table.forward(2, 1, 2)
+    turn_rows(6, 8)
+    first_table.forward(1, 3)
+    first_table.forward(2, 3)
     for q in range(3):
         columns(q + 1, near.at[q])
-    turn_rows(4, 6)
-    second_table.finish(0)
-    first_table.forward(1, 1)
-    turn_rows(6, 8)
-    first_table.finish(1)
-    first_table.forward(2, 1)
-    second_table.begin(1)
+    second_table.begin(0)
     acc[...] = jnp.zeros_like(acc)
-    first_table.finish(2)
+    for rnd in range(3):
+        first_table.finish(rnd)
+    second_table.sides(0)
     first_table.have()
-    second_table.forward(1, 0)
 
     def gather_rows(table, base, count, at):
         flat = table.reshape(16384, 2, 128)
@@ -287,13 +282,21 @@
     gather_tile(tab1, 0)
 
     def sum_tile(i, carry):
-        @pl.when(i == 1)
+        @pl.when(i == 0)
         def _():
-            second_table.second(1)
-
-        @pl.when(i == 6)
+            second_table.opposite(0)
+
+        @pl.when(i == 2)
         def _():
-            second_table.forward(1, 1)
+            second_table.forward(0, 0)
+
+        @pl.when(i == 4)
+        def _():
+            second_table.forward(0, 1, 2)
+
+        @pl.when(i == 7)
+        def _():
+            second_table.forward(0, 3)
 
         at = pl.multiple_of(i * TILE, TILE)
         fetched = got[...].reshape(TILE, 256).astype(F32)
@@ -342,40 +345,30 @@
 
     def scatter(p):
         to = lax.rem(row + p, ROWS)
-        return remote(
-            part.at[to, pl.ds(0, 17)], partgot.at[row, pl.ds(0, 17)], ps.at[p], pr.at[row], (to, sub)
-        )
-
-    def scattered(p):
-        source = lax.rem(row + p, ROWS)
-        return remote(
-            part.at[source, pl.ds(0, 17)], partgot.at[source, pl.ds(0, 17)], ps.at[p], pr.at[source],
-            (source, sub),
-        )
+        remote(
+            part.at[to, pl.ds(0, 17)], partgot.at[row, pl.ds(0, 17)], ps.at[0], pr.at[0], (to, sub)
+        ).start()
 
     def give(p):
         to = lax.rem(row + p, ROWS)
-        return remote(bchunk, rounded.at[row], bs.at[p], br.at[row], (to, sub))
-
-    def given(p):
-        source = lax.rem(row + p, ROWS)
-        return remote(bchunk, rounded.at[source], bs.at[p], br.at[source], (source, sub))
+        remote(bchunk, rounded.at[row], bs.at[0], br.at[0], (to, sub)).start()
 
     def publish(p):
         to = lax.rem(row + p, ROWS)
-        return remote(chunk, means.at[row], ms.at[p], mr.at[row], (to, sub))
-
-    def published(p):
-        source = lax.rem(row + p, ROWS)
-        return remote(chunk, means.at[source], ms.at[p], mr.at[source], (source, sub))
+        remote(chunk, means.at[row], ms.at[0], mr.at[0], (to, sub)).start()
+
+    def all_of(blocks, sem):
+        pltpu.make_async_copy(blocks, blocks, sem).wait()
+
+    others = pl.ds(0, ROWS - 1)
 
     def spread_books(p):
         to = (row, lax.rem(sub + p, SUBS))
-        return remote(rounded, every.at[sub], ys.at[p], yr.at[sub], to)
+        return remote(rounded, every.at[sub], ys.at[0], yr.at[sub], to)
 
     def spread_got(p):
         source = lax.rem(sub + p, SUBS)
-        return remote(rounded, every.at[source], ys.at[p], yr.at[source], (row, source))
+        return remote(rounded, every.at[source], ys.at[0], yr.at[source], (row, source))
 
     def column_copy(i):
         return pltpu.make_async_copy(
@@ -383,34 +376,32 @@
             vcol.at[lax.rem(i, 2)], vcsem.at[lax.rem(i, 2)],
         )
 
-    each(lambda p: scatter(p).start())
+    each(scatter)
     column_copy(0).start()
-    second_table.finish(1)
-
-    def add(p, value):
-        scattered(p).wait_recv()
-        return value + partgot[lax.rem(row + p, ROWS), :17, :]
-
-    value = lax.fori_loop(1, ROWS, add, part[row, :17, :])
+    partgot[row] = part[row]
+    first_table.drain()
+    second_table.finish(0)
+    all_of(partgot.at[others, pl.ds(0, 17)], pr.at[0])
+    value = jnp.sum(partgot[:, :17, :], axis=0)
     mean = value[:16, :] / value[16:17, :]
     chunk[...] = mean
     bchunk[...] = mean.astype(BF16)
     means[row] = mean
     rounded[row] = mean.astype(BF16)
-    each(lambda p: give(p).start())
+    each(give)
     second_table.have()
     gather_tile(tab2, 0)
-    each(lambda p: given(p).wait_recv())
+    each(publish)
+    all_of(rounded.at[others], br.at[0])
     every[sub] = rounded[...]
     for p in range(1, SUBS):
         spread_books(p).start()
-    each(lambda p: publish(p).start())
     own_codes.wait()
 
     def send_piece(p, r):
         s = lax.rem(sub + p, SUBS)
         return remote(
-            piece.at[r, p], piecegot.at[row], ws.at[p * 8 + r], wr.at[row], (sub * 8 + r, s)
+            piece.at[r, p], piecegot.at[row], ws.at[0], wr.at[0], (sub * 8 + r, s)
         )
 
     def to_me(p, r):
@@ -480,38 +471,44 @@
             else:
                 @pl.when(to_me(p, r))
                 def _():
-                    pltpu.make_async_copy(piece.at[r, p], piecegot.at[row], wr.at[row]).start()
+                    pltpu.make_async_copy(piece.at[r, p], piecegot.at[row], wr.at[0]).start()
 
                 @pl.when(jnp.logical_not(to_me(p, r)))
                 def _():
                     send_piece(p, r).start()
 
-    def collect(p, value):
-        source = lax.rem(row + p, ROWS)
-        pltpu.make_async_copy(piece.at[0, 0], piecegot.at[source], wr.at[source]).wait()
-        return value + piecegot[source].astype(F32)
-
-    cross[...] = lax.fori_loop(0, ROWS, collect, jnp.zeros(cross.shape, F32))
-
     for k in range(6):
         exchange(k).wait_send()
-    first_table.drain()
     second_table.drain()
-    for p in range(1, SUBS):
-        share_codes(p).wait_send()
-        spread_books(p).wait_send()
-    each(lambda p: published(p).wait_recv())
-    each(lambda p: scatter(p).wait_send())
-    each(lambda p: give(p).wait_send())
-    each(lambda p: publish(p).wait_send())
-    for p in range(SUBS):
-        for r in range(8):
-            if p:
-                send_piece(p, r).wait_send()
-            else:
-                @pl.when(jnp.logical_not(to_me(p, r)))
-                def _():
-                    send_piece(p, r).wait_send()
+    all_of(every_codes.at[pl.ds(0, SUBS - 1)], cs.at[0])
+    all_of(every.at[pl.ds(0, SUBS - 1)], ys.at[0])
+    all_of(partgot.at[others, pl.ds(0, 17)], ps.at[0])
+    all_of(rounded.at[others], bs.at[0])
+    all_of(means.at[others], ms.at[0])
+    all_of(means.at[others], mr.at[0])
+
+    def order(q, carry):
+        for half in range(2):
+            left, right = means[q * 4 + 2 * half], means[q * 4 + 2 * half + 1]
+            cols = slice(half * 128, half * 128 + 128)
+            outbooks[2 * q, :, cols] = jnp.where(lane < 64, left, pltpu.roll(right, 64, 1))
+            outbooks[2 * q + 1, :, cols] = jnp.where(lane < 64, pltpu.roll(left, 64, 1), right)
+        return carry
+
+    lax.fori_loop(0, 8, order, 0)
+    all_of(piecegot, wr.at[0])
+    value = jnp.zeros(cross.shape, F32)
+    for r in range(ROWS):
+        value = value + piecegot[r].astype(F32)
+    cross[...] = value
+
+    @pl.when(sub == block)
+    def _():
+        all_of(piecegot.at[others], ws.at[0])
+
+    @pl.when(sub != block)
+    def _():
+        all_of(piecegot, ws.at[0])
 
 
 def step_call(ids, vectors, centroids, rotation, codes):
@@ -520,7 +517,7 @@
     return pl.pallas_call(
         step_kernel,
         out_shape=(
-            jax.ShapeDtypeStruct((ROWS, 16, 128), F32),
+            jax.ShapeDtypeStruct((16, 16, 256), F32),
             jax.ShapeDtypeStruct((32, 256), F32),
         ),
         in_specs=[
@@ -542,6 +539,7 @@
             pltpu.VMEM((4, 272, 256), F32),
             pltpu.VMEM((ROWS, 24, 128), F32),
             pltpu.VMEM((ROWS, 24, 128), F32),
+            pltpu.VMEM((ROWS, 16, 128), F32),
             pltpu.VMEM((16, 128), F32),
             pltpu.VMEM((16, 128), BF16),
             pltpu.VMEM((ROWS, 16, 128), BF16),
@@ -554,14 +552,12 @@
             pltpu.VMEM((8, SUBS, 32, 256), BF16),
             pltpu.VMEM((ROWS, 32, 256), BF16),
             dma((2,)), dma((6,)), dma((6,)),
-            dma((6,)), dma((72,)), dma((72,)),
-            dma((4,)), dma((48,)), dma((48,)),
-            dma((SUBS,)), dma((SUBS,)),
-            dma((ROWS,)), dma((ROWS,)),
-            dma((ROWS,)), dma((ROWS,)),
-            dma((ROWS,)), dma((ROWS,)),
-            dma((SUBS,)), dma((SUBS,)),
-            dma((ROWS,)), dma((ROWS,)),
+            dma((6,)), dma((2,)), dma((120,)), dma((2,)),
+            dma((2,)), dma((2,)), dma((40,)), dma((2,)),
+            dma((1,)), dma((SUBS,)),
+            dma((1,)), dma((1,)), dma((1,)), dma((1,)), dma((1,)), dma((1,)),
+            dma((1,)), dma((SUBS,)),
+            dma((1,)), dma((1,)),
             dma((2,)),
         ],
         compiler_params=pltpu.CompilerParams(
@@ -584,11 +580,10 @@
     half = inner // 64
     block = jnp.where(half == 0, at_z * 4 + at_y, at_y * 4 + at_z)
     ids = (((at_core * 2 + half) * 16 + block) * 4 + near) * 64 + inner % 64
-    means, cross_cov = step_call(
+    books, cross_cov = step_call(
         ids, vectors, centroids, rotation, codes.reshape(2, 8, -1)
     )
-    codebooks = means.reshape(8, 4, 16, 2, 64).transpose(0, 3, 1, 4, 2).reshape(16, 256, 16)
-    return codebooks, cross_cov
+    return books.transpose(0, 2, 1), cross_cov
 
 
 def solution(mesh):

time: 147 us -> 131 us (0.89)
  Pallas kernels: 141 us -> 125 us
    pallas_call x1, Pallas kernels: 141 us -> 125 us  [step_call(): pl.pallas_call(step_kernel, out_shape=(jax.ShapeDtypeStruct((16, 16, 256)...]
    reshape x2 -> x0, local copies, waits for them, and re-layouts: 2.31 us -> none  [local(): means.reshape(8, 4, 16, 2, 64).transpose(0, 3, 1, 4, 2).reshape(16, 256, 16)]
    unnamed x1 -> x2, local copies, waits for them, and re-layouts: 1.37 us -> 3.05 us
where the time goes in v5:
time: 131 us; the launch traced here: 130 us
  Pallas kernels  125 us (95%)
  local copies, waits for them, and re-layouts  3.05 us (2%)
  other arithmetic  1.55 us (1%)
    pallas_call x1, Pallas kernels, step_call(): pl.pallas_call(step_kernel, out_shape=(jax.ShapeDtypeStruct((16, 16, 256)...  125 us
    unnamed x2, local copies, waits for them, and re-layouts  3.05 us

profile of v5, /device:TPU:7, one launch (start us, length us, event | category | flops | bytes accessed | tf_op | source)
XLA Modules:
  0.0 130.5 jit_solution(10994878156975097424)
XLA Ops:
  0.6 1.6 %fusion.7.ids = s32[8192]{0:T(1024)} fusion(s32[8192]{0:T(1024)} %param.6, s32[]{:T(128)S(6)} %axis_index.12), kind=kLoop, calls=%fused_computation.37 | loop fusion | flops 1040384 | bytes 65540 | tf_op jit(solution)/shard_map/add | solution.py:582
  2.2 125.2 %step.1 = (f32[16,16,256]{2,1,0:T(8,128)}, f32[32,256]{1,0:T(8,128)}) custom-call(s32[8192]{0:T(1024)} %fusion.7.ids, bf16[8192,1024]{1,0:T(8,128)(2,1)} %v.1, bf16[128,1024]{1,0:T(8,128)(2,1)} %c.1, bf16[1024,256]{1,0:T(8,128)(2,1)} %rot.1, s32[2,8,8192]{2,1,0:T(8,128)} %bitcast.3), custom_call_target="tpu_custom_call" | custom-call | flops 20000000000 | bytes 40000000 | tf_op jit(solution)/shard_map/step/pallas_call | solution.py:517
  127.4 1.7 %copy.9 = f32[16,256,16]{1,2,0:T(8,128)} copy(f32[16,256,16]{1,2,0:T(8,128)} %bitcast.2) | data formatting | bytes 524288
  129.1 1.4 %copy.10 = f32[32,256]{1,0:T(8,128)} copy(f32[32,256]{1,0:T(8,128)} %get-tuple-element.9) | data formatting | bytes 65536

commit v6 on v5

--- a/solution.py
+++ b/solution.py
@@ -22,7 +22,7 @@
 def step_kernel(
     ids, v, c, rot, codes, outbooks, cross,
     tab1, tab2, near, stage1, stage2, vbuf, vr, got, turned, acc, part, partgot, means,
-    chunk, bchunk, rounded, every, books, every_codes, resid, vcol, total, piece, piecegot,
+    chunk, bchunk, rounded, every, books, diagonal, every_codes, resid, vcol, total, piece, piecegot,
     vsem, xs, xr, l1, s1, r1, o1, l2, s2, r2, o2, cs, cr, ps, pr, ms, mr, bs, br, ys, yr, ws, wr,
     vcsem,
 ):
@@ -226,7 +226,7 @@
     for k in range(2):
         exchange(k).wait_recv()
         exchange(k + 4).start()
-    turn_rows(3, 4)
+    turn_rows(3, 5)
     first_table.forward(0, 0)
     exchange(2).wait_recv()
     exchange(3).wait_recv()
@@ -234,6 +234,7 @@
     project(2, near.at[1])
     first_table.begin(1)
     first_table.forward(0, 1, 2)
+    turn_rows(5, 6)
     exchange(4).wait_recv()
     exchange(5).wait_recv()
     project(3, near.at[2])
@@ -241,17 +242,16 @@
     first_table.sides(1)
     first_table.sides(2)
     first_table.forward(0, 3)
-    turn_rows(4, 5)
+    turn_rows(6, 7)
     first_table.opposite(1)
     first_table.opposite(2)
     for p in range(1, SUBS):
         share_codes(p).start()
-    turn_rows(5, 6)
+    turn_rows(7, 8)
     first_table.forward(1, 0)
     first_table.forward(2, 0)
     first_table.forward(1, 1, 2)
     first_table.forward(2, 1, 2)
-    turn_rows(6, 8)
     first_table.forward(1, 3)
     first_table.forward(2, 3)
     for q in range(3):
@@ -290,11 +290,15 @@
         def _():
             second_table.forward(0, 0)
 
+        @pl.when(i == 3)
+        def _():
+            second_table.forward(0, 1)
+
         @pl.when(i == 4)
         def _():
-            second_table.forward(0, 1, 2)
-
-        @pl.when(i == 7)
+            second_table.forward(0, 2)
+
+        @pl.when(i == 6)
         def _():
             second_table.forward(0, 3)
 
@@ -379,8 +383,8 @@
     each(scatter)
     column_copy(0).start()
     partgot[row] = part[row]
+    second_table.finish(0)
     first_table.drain()
-    second_table.finish(0)
     all_of(partgot.at[others, pl.ds(0, 17)], pr.at[0])
     value = jnp.sum(partgot[:, :17, :], axis=0)
     mean = value[:16, :] / value[16:17, :]
@@ -389,9 +393,9 @@
     means[row] = mean
     rounded[row] = mean.astype(BF16)
     each(give)
+    each(publish)
     second_table.have()
     gather_tile(tab2, 0)
-    each(publish)
     all_of(rounded.at[others], br.at[0])
     every[sub] = rounded[...]
     for p in range(1, SUBS):
@@ -413,15 +417,19 @@
             spread_got(p).wait_recv()
             shared_codes(p).wait_recv()
 
-        def relay(q, carry):
+        for q in range(6):
             for half in range(2):
                 left = every[s, q * 4 + 2 * half].astype(F32)
                 right = every[s, q * 4 + 2 * half + 1].astype(F32)
                 books[2 * q, half] = jnp.where(lane < 64, left, pltpu.roll(right, 64, 1))
                 books[2 * q + 1, half] = jnp.where(lane < 64, pltpu.roll(left, 64, 1), right)
-            return carry
-
-        lax.fori_loop(0, 8, relay, 0)
+        for q in range(2):
+            for l in range(4):
+                pair = every[s, 24 + q * 4 + l].astype(F32)
+                rows = slice(l * 16, l * 16 + 16)
+                diagonal[q, rows, :] = jnp.where(lane < 64, pair, 0.0).astype(BF16)
+                rows = slice(64 + l * 16, 64 + l * 16 + 16)
+                diagonal[q, rows, :] = jnp.where(lane < 64, 0.0, pair).astype(BF16)
         total[...] = jnp.zeros_like(total)
 
         def cross_tile(i, carry):
@@ -433,14 +441,14 @@
                     column_copy(i + 1).start()
 
                 fetched = got[...].reshape(TILE, 256).astype(F32)
-                value = (vcol[lax.rem(i, 2)].astype(F32) - fetched).T
-                resid[:, pl.ds(pl.multiple_of(i * TILE, TILE), TILE)] = value.astype(BF16)
+                value = vcol[lax.rem(i, 2)].astype(F32) - fetched
+                resid[pl.ds(pl.multiple_of(i * TILE, TILE), TILE), :] = value.astype(BF16)
                 ahead = jnp.minimum(i + 1, TILES - 1) * TILE
 
             for quarter in range(TILE // 256):
                 built = []
                 at = pl.multiple_of(i * TILE + quarter * 256, 256)
-                for m in range(16):
+                for m in range(12):
                     pieces = []
                     for t in range(2):
                         cols = pl.ds(pl.multiple_of(at + t * 128, 128), 128)
@@ -457,14 +465,32 @@
                             ))
                         pieces.append(jnp.concatenate(both, axis=0).astype(BF16))
                     built.append(jnp.concatenate(pieces, axis=1))
-                total[...] += nt(resid[:, pl.ds(at, 256)], jnp.concatenate(built, axis=0))
+                for g in range(2):
+                    code = [
+                        every_codes[s, 1, 4 + g * 2 + m:5 + g * 2 + m, pl.ds(at, 256)] for m in range(2)
+                    ]
+                    hot = [(high[:, :256] == (code[m] & 63)).astype(BF16) for m in range(2)]
+                    picked = jnp.dot(
+                        diagonal[g], jnp.concatenate(hot, axis=0), preferred_element_type=F32
+                    )
+                    for m in range(2):
+                        value = picked[m * 64:m * 64 + 16, :]
+                        for l in range(1, 4):
+                            other = picked[m * 64 + l * 16:m * 64 + (l + 1) * 16, :]
+                            value = jnp.where(code[m] >= l * 64, other, value)
+                        built.append(value.astype(BF16))
+                total[...] += jnp.dot(
+                    jnp.concatenate(built, axis=0), resid[pl.ds(at, 256), :],
+                    preferred_element_type=F32,
+                )
                 if p == 0:
                     gather_rows(tab2, ahead + quarter * 256, 256, quarter * 256)
             return carry
 
         lax.fori_loop(0, TILES, cross_tile, 0)
+        value = (total[...] * (1.0 / KS)).T.astype(BF16)
         for r in range(8):
-            piece[r, p] = (total[r * 32:(r + 1) * 32, :] * (1.0 / KS)).astype(BF16)
+            piece[r, p] = value[r * 32:(r + 1) * 32, :]
         for r in range(8):
             if p:
                 send_piece(p, r).start()
@@ -487,15 +513,12 @@
     all_of(means.at[others], ms.at[0])
     all_of(means.at[others], mr.at[0])
 
-    def order(q, carry):
+    for q in range(8):
         for half in range(2):
             left, right = means[q * 4 + 2 * half], means[q * 4 + 2 * half + 1]
             cols = slice(half * 128, half * 128 + 128)
             outbooks[2 * q, :, cols] = jnp.where(lane < 64, left, pltpu.roll(right, 64, 1))
             outbooks[2 * q + 1, :, cols] = jnp.where(lane < 64, pltpu.roll(left, 64, 1), right)
-        return carry
-
-    lax.fori_loop(0, 8, order, 0)
     all_of(piecegot, wr.at[0])
     value = jnp.zeros(cross.shape, F32)
     for r in range(ROWS):
@@ -544,9 +567,10 @@
             pltpu.VMEM((16, 128), BF16),
             pltpu.VMEM((ROWS, 16, 128), BF16),
             pltpu.VMEM((SUBS, ROWS, 16, 128), BF16),
-            pltpu.VMEM((16, 2, 16, 128), F32),
+            pltpu.VMEM((12, 2, 16, 128), F32),
+            pltpu.VMEM((2, 128, 128), BF16),
             pltpu.VMEM((SUBS, 2, 8, TILE * TILES), I32),
-            pltpu.VMEM((256, TILE * TILES), BF16),
+            pltpu.VMEM((TILE * TILES, 256), BF16),
             pltpu.VMEM((2, TILE, 256), BF16),
             pltpu.VMEM((256, 256), F32),
             pltpu.VMEM((8, SUBS, 32, 256), BF16),

time: 131 us -> 128 us (0.977)
  Pallas kernels: 125 us -> 122 us
    pallas_call x1, Pallas kernels: 125 us -> 122 us  [step_call(): pl.pallas_call(step_kernel, out_shape=(jax.ShapeDtypeStruct((16, 16, 256)...]
where the time goes in v6:
time: 128 us; the launch traced here: 127 us
  Pallas kernels  122 us (95%)
  local copies, waits for them, and re-layouts  3.05 us (2%)
  other arithmetic  1.55 us (1%)
    pallas_call x1, Pallas kernels, step_call(): pl.pallas_call(step_kernel, out_shape=(jax.ShapeDtypeStruct((16, 16, 256)...  122 us
    unnamed x2, local copies, waits for them, and re-layouts  3.05 us

profile of v6, /device:TPU:7, one launch (start us, length us, event | category | flops | bytes accessed | tf_op | source)
XLA Modules:
  0.0 127.2 jit_solution(10513221023232807888)
XLA Ops:
  0.6 1.6 %fusion.7.ids = s32[8192]{0:T(1024)} fusion(s32[8192]{0:T(1024)} %param.6, s32[]{:T(128)S(6)} %axis_index.12), kind=kLoop, calls=%fused_computation.37 | loop fusion | flops 1040384 | bytes 65540 | tf_op jit(solution)/shard_map/add | solution.py:606
  2.2 122.0 %step.1 = (f32[16,16,256]{2,1,0:T(8,128)}, f32[32,256]{1,0:T(8,128)}) custom-call(s32[8192]{0:T(1024)} %fusion.7.ids, bf16[8192,1024]{1,0:T(8,128)(2,1)} %v.1, bf16[128,1024]{1,0:T(8,128)(2,1)} %c.1, bf16[1024,256]{1,0:T(8,128)(2,1)} %rot.1, s32[2,8,8192]{2,1,0:T(8,128)} %bitcast.3), custom_call_target="tpu_custom_call" | custom-call | flops 20000000000 | bytes 40000000 | tf_op jit(solution)/shard_map/step/pallas_call | solution.py:540
  124.2 1.7 %copy.9 = f32[16,256,16]{1,2,0:T(8,128)} copy(f32[16,256,16]{1,2,0:T(8,128)} %bitcast.2) | data formatting | bytes 524288
  125.9 1.4 %copy.10 = f32[32,256]{1,0:T(8,128)} copy(f32[32,256]{1,0:T(8,128)} %get-tuple-element.9) | data formatting | bytes 65536

commit v7 on v6

--- a/solution.py
+++ b/solution.py
@@ -282,23 +282,23 @@
     gather_tile(tab1, 0)
 
     def sum_tile(i, carry):
-        @pl.when(i == 0)
+        @pl.when(i == 1)
         def _():
             second_table.opposite(0)
 
-        @pl.when(i == 2)
+        @pl.when(i == 3)
         def _():
             second_table.forward(0, 0)
 
-        @pl.when(i == 3)
+        @pl.when(i == 4)
         def _():
             second_table.forward(0, 1)
 
-        @pl.when(i == 4)
+        @pl.when(i == 5)
         def _():
             second_table.forward(0, 2)
 
-        @pl.when(i == 6)
+        @pl.when(i == 7)
         def _():
             second_table.forward(0, 3)
 
@@ -383,9 +383,9 @@
     each(scatter)
     column_copy(0).start()
     partgot[row] = part[row]
-    second_table.finish(0)
     first_table.drain()
     all_of(partgot.at[others, pl.ds(0, 17)], pr.at[0])
+    second_table.finish(0)
     value = jnp.sum(partgot[:, :17, :], axis=0)
     mean = value[:16, :] / value[16:17, :]
     chunk[...] = mean

time: 128 us -> 126 us (0.984)
  Pallas kernels: 122 us -> 120 us
    pallas_call x1, Pallas kernels: 122 us -> 120 us  [step_call(): pl.pallas_call(step_kernel, out_shape=(jax.ShapeDtypeStruct((16, 16, 256)...]
where the time goes in v7:
time: 126 us; the launch traced here: 125 us
  Pallas kernels  120 us (95%)
  local copies, waits for them, and re-layouts  3.05 us (2%)
  other arithmetic  1.55 us (1%)
    pallas_call x1, Pallas kernels, step_call(): pl.pallas_call(step_kernel, out_shape=(jax.ShapeDtypeStruct((16, 16, 256)...  120 us
    unnamed x2, local copies, waits for them, and re-layouts  3.05 us

profile of v7, /device:TPU:7, one launch (start us, length us, event | category | flops | bytes accessed | tf_op | source)
XLA Modules:
  0.0 125.2 jit_solution(13435895418515953080)
XLA Ops:
  0.6 1.6 %fusion.7.ids = s32[8192]{0:T(1024)} fusion(s32[8192]{0:T(1024)} %param.6, s32[]{:T(128)S(6)} %axis_index.12), kind=kLoop, calls=%fused_computation.37 | loop fusion | flops 1040384 | bytes 65540 | tf_op jit(solution)/shard_map/add | solution.py:606
  2.2 120.0 %step.1 = (f32[16,16,256]{2,1,0:T(8,128)}, f32[32,256]{1,0:T(8,128)}) custom-call(s32[8192]{0:T(1024)} %fusion.7.ids, bf16[8192,1024]{1,0:T(8,128)(2,1)} %v.1, bf16[128,1024]{1,0:T(8,128)(2,1)} %c.1, bf16[1024,256]{1,0:T(8,128)(2,1)} %rot.1, s32[2,8,8192]{2,1,0:T(8,128)} %bitcast.3), custom_call_target="tpu_custom_call" | custom-call | flops 20000000000 | bytes 40000000 | tf_op jit(solution)/shard_map/step/pallas_call | solution.py:540
  122.2 1.7 %copy.9 = f32[16,256,16]{1,2,0:T(8,128)} copy(f32[16,256,16]{1,2,0:T(8,128)} %bitcast.2) | data formatting | bytes 524288
  123.8 1.4 %copy.10 = f32[32,256]{1,0:T(8,128)} copy(f32[32,256]{1,0:T(8,128)} %get-tuple-element.9) | data formatting | bytes 65536

commit v8 on v7

--- a/solution.py
+++ b/solution.py
@@ -256,12 +256,12 @@
     first_table.forward(2, 3)
     for q in range(3):
         columns(q + 1, near.at[q])
-    second_table.begin(0)
     acc[...] = jnp.zeros_like(acc)
     for rnd in range(3):
         first_table.finish(rnd)
+    second_table.begin(0)
+    first_table.have()
     second_table.sides(0)
-    first_table.have()
 
     def gather_rows(table, base, count, at):
         flat = table.reshape(16384, 2, 128)

time: 126 us -> 128 us (1.016)
  Pallas kernels: 120 us -> 122 us
    pallas_call x1, Pallas kernels: 120 us -> 122 us  [step_call(): pl.pallas_call(step_kernel, out_shape=(jax.ShapeDtypeStruct((16, 16, 256)...]
where the time goes in v8:
time: 128 us; the launch traced here: 127 us
  Pallas kernels  122 us (95%)
  local copies, waits for them, and re-layouts  3.05 us (2%)
  other arithmetic  1.55 us (1%)
    pallas_call x1, Pallas kernels, step_call(): pl.pallas_call(step_kernel, out_shape=(jax.ShapeDtypeStruct((16, 16, 256)...  122 us
    unnamed x2, local copies, waits for them, and re-layouts  3.05 us

profile of v8, /device:TPU:7, one launch (start us, length us, event | category | flops | bytes accessed | tf_op | source)
XLA Modules:
  0.0 127.0 jit_solution(9830099620789241594)
XLA Ops:
  0.6 1.6 %fusion.7.ids = s32[8192]{0:T(1024)} fusion(s32[8192]{0:T(1024)} %param.6, s32[]{:T(128)S(6)} %axis_index.12), kind=kLoop, calls=%fused_computation.37 | loop fusion | flops 1040384 | bytes 65540 | tf_op jit(solution)/shard_map/add | solution.py:606
  2.2 121.7 %step.1 = (f32[16,16,256]{2,1,0:T(8,128)}, f32[32,256]{1,0:T(8,128)}) custom-call(s32[8192]{0:T(1024)} %fusion.7.ids, bf16[8192,1024]{1,0:T(8,128)(2,1)} %v.1, bf16[128,1024]{1,0:T(8,128)(2,1)} %c.1, bf16[1024,256]{1,0:T(8,128)(2,1)} %rot.1, s32[2,8,8192]{2,1,0:T(8,128)} %bitcast.3), custom_call_target="tpu_custom_call" | custom-call | flops 20000000000 | bytes 40000000 | tf_op jit(solution)/shard_map/step/pallas_call | solution.py:540
  123.9 1.7 %copy.9 = f32[16,256,16]{1,2,0:T(8,128)} copy(f32[16,256,16]{1,2,0:T(8,128)} %bitcast.2) | data formatting | bytes 524288
  125.6 1.4 %copy.10 = f32[32,256]{1,0:T(8,128)} copy(f32[32,256]{1,0:T(8,128)} %get-tuple-element.9) | data formatting | bytes 65536
